TPU v7x, 32 devices: a whole 2x2x4 slice. The times are simulated.
32 devices in a mesh: theta: 4 (over y, core), phi: 8 (over z, x).
Axes of the slice: x: 2, y: 2, z: 4, core: 2. Of those that a mesh axis runs over, the one named last changes fastest.
Arguments:
- density: float32 [2, 32, 768, 128], P(None, 'theta', 'phi'), may hold values from 0.5 to 2
- velocity: float32 [3, 32, 768, 128], P(None, 'theta', 'phi'), may hold values from -3 to 3
- bfield: float32 [3, 32, 768, 128], P(None, 'theta', 'phi'), may hold values from -6 to 6
- levels: int32 [2, 4], replicated, may hold values from 0 to 3
Outputs:
- density_new: float32 [2, 32, 768, 128], P(None, 'theta', 'phi')
- bfield_new: float32 [3, 32, 768, 128], P(None, 'theta', 'phi')
Inputs may be any that keep to these rules, and one draw needn't show every extreme that they name: `levels`: a row at level l keeps the azimuthal modes below 128 // 2**l.
All inputs are finite; a program needn't handle non-finite values.
Results may differ from a plain program's by a relative error of at most 0.00007.
Values sent between devices are 32-bit elements; how exact they have to be, the bound alone decides.
A program may use at most 64 MiB of HBM per device.

v0:
```python
import math

import jax
import jax.numpy as jnp
from jax import lax
from jax.sharding import PartitionSpec as P

CAP = 4
KMAX = 128


TIME_STEP = 0.2
PARITY = (1.0, 1.0, 1.0, -1.0, -1.0, 1.0, -1.0, -1.0)


def shifted_2(block, axis, distance):
    devices = range(lax.axis_size(axis))
    route = [((i - distance) % len(devices), i) for i in devices]
    return lax.ppermute(block, axis, route)


def with_halo(cells, sides, width, closed):
    for axis, dim in sides:
        count = lax.axis_size(axis)
        ends = count if closed else count - 1
        head = lax.slice_in_dim(cells, 0, width, axis=dim)
        tail = lax.slice_in_dim(cells, cells.shape[dim] - width, cells.shape[dim], axis=dim)
        cells = jnp.concatenate(
            [
                lax.ppermute(tail, axis, [(i, (i + 1) % count) for i in range(ends)]),
                cells,
                lax.ppermute(head, axis, [((i + 1) % count, i) for i in range(ends)]),
            ],
            axis=dim,
        )
    return cells


def window_of(array, spans):
    return array[spans[0][0] : spans[0][1], spans[1][0] : spans[1][1], spans[2][0] : spans[2][1]]


def moved(spans, direction, start, length):
    return tuple(
        ((start, start + length) if other == direction else spans[other] for other in range(3))
    )


def corner_mean(field, extents, first_axis, second_axis):
    base = [(1, extents[0] + 1), (1, extents[1] + 1), (1, extents[2] + 1)]
    total = jnp.zeros((), jnp.float32)
    for first_start in (0, 1):
        for second_start in (0, 1):
            spans_now = list(base)
            spans_now[first_axis] = (first_start, first_start + extents[first_axis] + 1)
            spans_now[second_axis] = (second_start, second_start + extents[second_axis] + 1)
            total = total + window_of(field, spans_now)
    return 0.25 * total


def advance(extended):
    extents = (extended.shape[1] - 4, extended.shape[2] - 4, extended.shape[3] - 4)
    inner_span = tuple(((2, extent + 2) for extent in extents))
    speed_for = (3, 4, 2)
    densities = []
    for channel in range(2):
        amount = extended[channel]
        tendency = jnp.zeros(extents, jnp.float32)
        for direction in range(3):
            extent_now = extents[direction]
            lower_span = moved(inner_span, direction, 1, extent_now + 1)
            upper_span = moved(inner_span, direction, 2, extent_now + 1)
            speed_field = extended[speed_for[direction]]
            left_amount = window_of(amount, lower_span)
            right_amount = window_of(amount, upper_span)
            left_speed = window_of(speed_field, lower_span)
            right_speed = window_of(speed_field, upper_span)
            fluxes = 0.5 * (
                left_amount * left_speed + right_amount * right_speed
            ) - 0.5 * jnp.maximum(jnp.abs(left_speed), jnp.abs(right_speed)) * (
                right_amount - left_amount
            )
            tendency = (
                tendency
                + lax.slice_in_dim(fluxes, 1, extent_now + 1, axis=direction)
                - lax.slice_in_dim(fluxes, 0, extent_now, axis=direction)
            )
        densities.append(window_of(amount, inner_span) - TIME_STEP * tendency)
    wide_span = tuple(((1, extent + 3) for extent in extents))
    axis_of = (2, 0, 1)
    centred = []
    for component in range(3):
        direction = axis_of[component]
        shifted = moved(wide_span, direction, 2, extents[direction] + 2)
        face_field = extended[5 + component]
        centred.append(0.5 * (window_of(face_field, wide_span) + window_of(face_field, shifted)))
    speeds = [window_of(extended[2 + component], wide_span) for component in range(3)]
    emf_radial = -(speeds[1] * centred[2] - speeds[2] * centred[1])
    emf_theta = -(speeds[2] * centred[0] - speeds[0] * centred[2])
    emf_phi = -(speeds[0] * centred[1] - speeds[1] * centred[0])
    edge_phi = corner_mean(emf_phi, extents, 0, 2)
    edge_theta = corner_mean(emf_theta, extents, 1, 2)
    edge_radial = corner_mean(emf_radial, extents, 0, 1)
    radial_len = extents[2]
    inner_faces = [window_of(extended[5 + component], inner_span) for component in range(3)]
    new_radial = inner_faces[0] - TIME_STEP * (
        edge_phi[1:, :, :radial_len]
        - edge_phi[:-1, :, :radial_len]
        - (edge_theta[:, 1:, :radial_len] - edge_theta[:, :-1, :radial_len])
    )
    new_theta = inner_faces[1] - TIME_STEP * (
        edge_radial[:-1, 1:, :]
        - edge_radial[:-1, :-1, :]
        - (edge_phi[:-1, :, 1:] - edge_phi[:-1, :, :-1])
    )
    new_phi = inner_faces[2] - TIME_STEP * (
        edge_theta[:, :-1, 1:]
        - edge_theta[:, :-1, :-1]
        - (edge_radial[1:, :-1, :] - edge_radial[:-1, :-1, :])
    )
    return (jnp.stack(densities), jnp.stack([new_radial, new_theta, new_phi]))


def fourier_table(cycle_len, orders_kept):
    points = jnp.arange(cycle_len, dtype=jnp.int32)[:, None]
    orders = jnp.arange(orders_kept, dtype=jnp.int32)[None, :]
    phase = points * orders % cycle_len
    angle = phase.astype(jnp.float32) * (2.0 * math.pi / cycle_len)
    return jnp.concatenate([jnp.cos(angle), jnp.sin(angle)], axis=1)


def local(density, velocity, bfield, levels):
    combined = jnp.concatenate([density, velocity, bfield], axis=0)
    channels, theta_len, phi_len, radial_len = combined.shape
    theta_count = lax.axis_size("theta")
    phi_count = lax.axis_size("phi")
    theta_index = lax.axis_index("theta")
    phi_index = lax.axis_index("phi")
    at_north = theta_index == 0
    at_south = theta_index == theta_count - 1
    edge_rows = jnp.where(at_north, combined[:, :CAP], combined[:, theta_len - CAP :])
    slot_rows = edge_rows.reshape(channels * CAP, phi_len, radial_len)
    cycle_rows = lax.all_to_all(slot_rows, "phi", split_axis=0, concat_axis=1, tiled=True)
    per_device = cycle_rows.shape[0]
    cycle_len = cycle_rows.shape[1]
    fourier = fourier_table(cycle_len, KMAX)
    pole_pick = jnp.where(at_north, 0, 1).astype(jnp.int32)
    level_row = lax.dynamic_index_in_dim(levels, pole_pick, 0, keepdims=False)
    slot_ids = phi_index * per_device + jnp.arange(per_device, dtype=jnp.int32)
    row_ids = slot_ids % CAP
    slot_levels = jnp.sum(
        jnp.where(
            row_ids[:, None] == jnp.arange(CAP, dtype=jnp.int32)[None, :], level_row[None, :], 0
        ),
        axis=1,
    )
    limits = jnp.right_shift(jnp.int32(KMAX), slot_levels)
    column_order = jnp.arange(2 * KMAX, dtype=jnp.int32) % KMAX
    column_weight = jnp.where(column_order == 0, 1.0 / cycle_len, 2.0 / cycle_len).astype(
        jnp.float32
    )
    kept_weight = jnp.where(column_order[None, :] < limits[:, None], column_weight[None, :], 0.0)
    coeffs = jnp.einsum("spr,pm->smr", cycle_rows, fourier, precision=lax.Precision.HIGHEST)
    coeffs = coeffs * kept_weight[:, :, None]
    filtered = jnp.einsum("smr,pm->spr", coeffs, fourier, precision=lax.Precision.HIGHEST)
    parity = jnp.array(PARITY, jnp.float32)
    returned = lax.all_to_all(filtered, "phi", split_axis=1, concat_axis=0, tiled=True)
    cap_rows = returned.reshape(channels, CAP, phi_len, radial_len)
    north_version = jnp.concatenate([cap_rows, combined[:, CAP:]], axis=1)
    south_version = jnp.concatenate([combined[:, : theta_len - CAP], cap_rows], axis=1)
    combined = jnp.where(at_north, north_version, jnp.where(at_south, south_version, combined))
    pole_rows = jnp.concatenate([combined[:, :1], combined[:, theta_len - 2 :]], axis=1)
    received = shifted_2(pole_rows, "phi", phi_count // 2)
    column_parity = parity[:, None, None]
    ghost_north = received[:, 0] * column_parity
    ghost_first = received[:, 2] * column_parity
    ghost_second = received[:, 1] * column_parity
    widened = with_halo(combined, (("theta", 1),), 2, False)
    row_place = jnp.arange(theta_len + 4, dtype=jnp.int32)[None, :, None, None]
    widened = jnp.where(at_north & (row_place == 1), ghost_north[:, None], widened)
    widened = jnp.where(at_south & (row_place == theta_len + 2), ghost_first[:, None], widened)
    widened = jnp.where(at_south & (row_place == theta_len + 3), ghost_second[:, None], widened)
    wrapped = with_halo(widened, (("phi", 2),), 2, True)
    padded = jnp.pad(wrapped, ((0, 0), (0, 0), (0, 0), (2, 2)), mode="edge")
    return advance(padded)


def solution(mesh):
    return jax.shard_map(
        local,
        mesh=mesh,
        in_specs=(
            P(None, "theta", "phi", None),
            P(None, "theta", "phi", None),
            P(None, "theta", "phi", None),
            P(),
        ),
        out_specs=(P(None, "theta", "phi", None), P(None, "theta", "phi", None)),
        check_vma=False,
    )
```

profile of v0, /device:TPU:0, one launch (start us, length us, event | category | flops | bytes accessed | tf_op | source)
XLA Modules:
  0.0 204.7 jit_solution(9071225405337986467)
XLA Ops:
  0.7 1.2 constant_dynamic-update-slice_fusion.2
  1.9 1.4 constant_dynamic-update-slice_fusion.1
  3.6 2.5 %fusion.43 = (f32[8,4,96,128]{3,2,1,0:T(8,128)}, f32[8,4,96,128]{3,2,1,0:T(8,128)}, f32[8,4,96,128]{3,2,1,0:T(8,128)}) fusion(f32[8,8,96,128]{3,2,1,0:T(8,128)S(1)} %constant_dynamic-update-slice_fusion, pred[]{:T(512)S(6)} %eq.59), kind=kLoop, calls=%fused_computation.125 | loop fusion | flops 393216 | bytes 7864321 | tf_op jit(solution)/shard_map/slice | solution.py:141
  6.1 7.3 %all-to-all-start = ((f32[32,96,128]{2,1,0:T(8,128)}), f32[32,96,128]{2,1,0:T(8,128)}, u32[]{:S(2)}, u32[]{:S(2)}) async-start(f32[32,96,128]{2,1,0:T(8,128)} %bitcast.63), calls=%async_computation | async-start | bytes 3145728 | tf_op jit(solution)/shard_map/all_to_all | solution.py:143
  13.6 2.4 %fusion.34 = (f32[768,128]{0,1:T(8,128)S(1)}, f32[768,128]{0,1:T(8,128)}) fusion(), kind=kLoop, calls=%fused_computation.100 | loop fusion | flops 884736 | bytes 786432 | tf_op jit(solution)/shard_map/sin | solution.py:129
  16.0 34.4 %all-to-all-done = f32[32,96,128]{2,1,0:T(8,128)} async-done(((f32[32,96,128]{2,1,0:T(8,128)}), f32[32,96,128]{2,1,0:T(8,128)}, u32[]{:S(2)}, u32[]{:S(2)}) %all-to-all-start) | async-done | bytes 1572896 | tf_op jit(solution)/shard_map/all_to_all | solution.py:143
  50.4 1.6 copy.44
  52.0 1.5 fusion.2
  53.5 1.4 convolution_bitcast_fusion
  55.0 2.2 %copy.46 = f32[4,768,128]{2,0,1:T(4,128)} copy(f32[4,768,128]{2,1,0:T(8,128)S(1)} %convolution_bitcast_fusion) | data formatting | bytes 3145728 | tf_op jit(solution)/shard_map/smr,pm->spr/transpose | solution.py:165
  57.2 4.3 %all-to-all-start.1 = ((f32[4,768,128]{2,0,1:T(4,128)}), f32[4,768,128]{2,0,1:T(4,128)}, u32[]{:S(2)}, u32[]{:S(2)}) async-start(f32[4,768,128]{2,0,1:T(4,128)} %copy.46), calls=%async_computation.1 | async-start | bytes 3145728 | tf_op jit(solution)/shard_map/all_to_all | solution.py:167
  61.5 36.6 %all-to-all-done.1 = f32[4,768,128]{2,0,1:T(4,128)} async-done(((f32[4,768,128]{2,0,1:T(4,128)}), f32[4,768,128]{2,0,1:T(4,128)}, u32[]{:S(2)}, u32[]{:S(2)}) %all-to-all-start.1) | async-done | bytes 1572896 | tf_op jit(solution)/shard_map/all_to_all | solution.py:167
  98.1 1.7 copy.60
  101.7 1.3 collective-permute-start.2
  103.0 3.1 %collective-permute-start.1 = (f32[8,2,96,128]{3,2,1,0:T(8,128)S(1)}, f32[8,2,96,128]{3,2,1,0:T(8,128)S(1)}, u32[]{:S(2)}, u32[]{:S(2)}) collective-permute-start(f32[8,2,96,128]{3,2,1,0:T(8,128)S(1)} %get-tuple-element.16), channel_id=1, source_target_pairs={{0,8},{8,16},{16,24},{1,9},{9,17},{17,25},{2,10},{10,18},{18,26},{... | collective-permute-start | bytes 2359304 | tf_op jit(solution)/shard_map/ppermute | solution.py:30
  106.1 47.9 %collective-permute-done = f32[8,3,96,128]{3,2,1,0:T(8,128)S(1)} collective-permute-done((f32[8,3,96,128]{3,2,1,0:T(8,128)S(1)}, f32[8,3,96,128]{3,2,1,0:T(8,128)S(1)}, u32[]{:S(2)}, u32[]{:S(2)}) %collective-permute-start) | collective-permute-done | bytes 1179680 | tf_op jit(solution)/shard_map/ppermute | solution.py:19
  154.3 1.2 fusion.1
  155.6 2.1 %collective-permute-start.3 = (f32[8,12,2,128]{3,2,1,0:T(2,128)S(1)}, f32[8,12,2,128]{3,2,1,0:T(2,128)S(1)}, u32[]{:S(2)}, u32[]{:S(2)}) collective-permute-start(f32[8,12,2,128]{3,2,1,0:T(2,128)S(1)} %get-tuple-element.14), channel_id=1, source_target_pairs={{0,1},{1,2},{2,3},{3,4},{4,5},{5,6},{6,7},{7,0},{8,9},{9,10},{10,1... | collective-permute-start | bytes 294920 | tf_op jit(solution)/shard_map/ppermute | solution.py:30
  157.6 2.7 %collective-permute-start.4 = (f32[8,12,2,128]{3,2,1,0:T(2,128)S(1)}, f32[8,12,2,128]{3,2,1,0:T(2,128)S(1)}, u32[]{:S(2)}, u32[]{:S(2)}) collective-permute-start(f32[8,12,2,128]{3,2,1,0:T(2,128)S(1)} %get-tuple-element.15), channel_id=1, source_target_pairs={{1,0},{2,1},{3,2},{4,3},{5,4},{6,5},{7,6},{0,7},{9,8},{10,9},{11,1... | collective-permute-start | bytes 294920 | tf_op jit(solution)/shard_map/ppermute | solution.py:32
  160.3 2.6 %collective-permute-done.3 = f32[8,12,2,128]{3,2,1,0:T(2,128)S(1)} collective-permute-done((f32[8,12,2,128]{3,2,1,0:T(2,128)S(1)}, f32[8,12,2,128]{3,2,1,0:T(2,128)S(1)}, u32[]{:S(2)}, u32[]{:S(2)}) %collective-permute-start.3) | collective-permute-done | bytes 98336 | tf_op jit(solution)/shard_map/ppermute | solution.py:30
  163.0 1.2 collective-permute-done.4
  165.0 5.5 %fusion.40 = (f32[8,12,100,1]{3,2,1,0:T(8,128)}, f32[8,12,100,1]{3,2,1,0:T(8,128)}) fusion(f32[8,12,100,128]{3,2,1,0:T(8,128)S(1)} %pad_maximum_fusion.1), kind=kLoop, calls=%fused_computation.122 | loop fusion | bytes 153600 | tf_op jit(solution)/shard_map/jit(_pad)/slice | solution.py:184
  170.5 3.8 %copy.57 = f32[8,12,100,1]{2,1,0,3:T(8,128)S(1)} copy(f32[8,12,100,1]{3,2,1,0:T(8,128)} %get-tuple-element.12) | data formatting | bytes 76800 | tf_op jit(solution)/shard_map/jit(_pad)/slice | solution.py:184
  174.3 3.9 %copy.58 = f32[8,12,100,1]{2,1,0,3:T(8,128)S(1)} copy(f32[8,12,100,1]{3,2,1,0:T(8,128)} %get-tuple-element.13) | data formatting | bytes 76800 | tf_op jit(solution)/shard_map/jit(_pad)/slice | solution.py:184
  178.3 1.5 reshape.114
  179.8 1.5 reshape.113
  181.3 8.4 %pad_maximum_fusion = f32[8,12,100,132]{3,2,1,0:T(8,128)} fusion(f32[8,12,100,2]{3,2,1,0:T(8,128)S(1)} %reshape.114, f32[8,12,2,128]{3,2,1,0:T(2,128)S(1)} %collective-permute-done.4, f32[8,12,96,128]{3,2,1,0:T(8,128)S(1)} %bitcast.61, f32[8,12,2,128]{3,2,1,0:T(2,128)S(1)} %collective-permute-done.3, f32[8,12,100,2]{3,2,1,0:T(8,128)S(1)} %reshape.113), kind=kLoop, calls=%fused_computation | loop fusion | flops 5068800 | bytes 10137600 | tf_op jit(solution)/shard_map/jit(_pad)/concatenate | solution.py:184
  189.7 4.6 %slice_bitcast_fusion.2 = (f32[12,100,132]{2,1,0:T(8,128)S(1)}, f32[12,100,132]{2,1,0:T(8,128)S(1)}, f32[12,100,132]{2,1,0:T(8,128)S(1)}, f32[12,100,132]{2,1,0:...) fusion(f32[8,12,100,132]{3,2,1,0:T(8,128)} %pad_maximum_fusion), kind=kLoop, calls=%fused_computation.11 | loop fusion | bytes 10137600 | tf_op jit(solution)/shard_map/squeeze | solution.py:105
  195.8 1.3 multiply_subtract_fusion.1
  197.0 2.6 %subtract_negate_fusion.2 = (f32[10,98,130]{2,1,0:T(8,128)S(1)}, f32[10,98,130]{2,1,0:T(8,128)S(1)}, f32[10,98,130]{2,1,0:T(8,128)S(1)}) fusion(f32[12,100,132]{2,1,0:T(8,128)S(1)} %get-tuple-element.10, f32[12,100,132]{2,1,0:T(8,128)S(1)} %get-tuple-element.8, f32[12,100,132]{2,1,0:T(8,128)S(1)} %get-tuple-element.6, ...), kind=kLoop, calls=%fused_computation.29 | loop fusion | flops 2293200 | bytes 6115200 | tf_op jit(solution)/shard_map/neg | solution.py:100
  202.0 0.9 pad_maximum_fusion.4
  203.6 1.1 pad_maximum_fusion.3
  (49 shorter events, 7.9 us)
Async XLA Ops:
  0.6 12.7 %copy-start = (s32[2,4]{1,0:T(2,128)S(1)}, s32[2,4]{1,0:T(2,128)}, u32[]{:S(2)}) copy-start(s32[2,4]{1,0:T(2,128)} %param.8) | copy-start | bytes 100
  1.8 1.6 copy-start.6
  6.1 44.4 %all-to-all-start = ((f32[32,96,128]{2,1,0:T(8,128)}), f32[32,96,128]{2,1,0:T(8,128)}, u32[]{:S(2)}, u32[]{:S(2)}) async-start(f32[32,96,128]{2,1,0:T(8,128)} %bitcast.63), calls=%async_computation | async-start | bytes 3145728 | tf_op jit(solution)/shard_map/all_to_all | solution.py:143
  50.4 1.6 copy-start.5
  57.2 40.9 %all-to-all-start.1 = ((f32[4,768,128]{2,0,1:T(4,128)}), f32[4,768,128]{2,0,1:T(4,128)}, u32[]{:S(2)}, u32[]{:S(2)}) async-start(f32[4,768,128]{2,0,1:T(4,128)} %copy.46), calls=%async_computation.1 | async-start | bytes 3145728 | tf_op jit(solution)/shard_map/all_to_all | solution.py:167
  98.1 1.9 copy-start.3
  98.1 2.4 %copy-start.4 = (f32[8,4,96,128]{3,2,1,0:T(8,128)S(1)}, f32[8,4,96,128]{3,2,1,0:T(8,128)}, u32[]{:S(2)}) copy-start(f32[8,4,96,128]{3,2,1,0:T(8,128)} %get-tuple-element.20) | copy-start | bytes 4718596
  101.5 52.5 %copy-start.7 = (f32[8]{0:T(128)S(1)}, f32[8]{0:T(128)}, u32[]{:S(2)}) copy-start(f32[8]{0:T(128)} %constant.86.clone) | copy-start | bytes 100
  101.6 52.4 %collective-permute-start = (f32[8,3,96,128]{3,2,1,0:T(8,128)S(1)}, f32[8,3,96,128]{3,2,1,0:T(8,128)S(1)}, u32[]{:S(2)}, u32[]{:S(2)}) collective-permute-start(f32[8,3,96,128]{3,2,1,0:T(8,128)S(1)} %pad_maximum_fusion.2), channel_id=1, source_target_pairs={{4,0},{5,1},{6,2},{7,3},{0,4},{1,5},{2,6},{3,7},{12,8},{13,9},{14,... | collective-permute-start | bytes 3538952 | tf_op jit(solution)/shard_map/ppermute | solution.py:19
  101.7 52.5 %collective-permute-start.2 = (f32[8,2,96,128]{3,2,1,0:T(8,128)S(1)}, f32[8,2,96,128]{3,2,1,0:T(8,128)S(1)}, u32[]{:S(2)}, u32[]{:S(2)}) collective-permute-start(f32[8,2,96,128]{3,2,1,0:T(8,128)S(1)} %get-tuple-element.17), channel_id=1, source_target_pairs={{8,0},{16,8},{24,16},{9,1},{17,9},{25,17},{10,2},{18,10},{26,18},{... | collective-permute-start | bytes 2359304 | tf_op jit(solution)/shard_map/ppermute | solution.py:32
  103.0 51.2 %collective-permute-start.1 = (f32[8,2,96,128]{3,2,1,0:T(8,128)S(1)}, f32[8,2,96,128]{3,2,1,0:T(8,128)S(1)}, u32[]{:S(2)}, u32[]{:S(2)}) collective-permute-start(f32[8,2,96,128]{3,2,1,0:T(8,128)S(1)} %get-tuple-element.16), channel_id=1, source_target_pairs={{0,8},{8,16},{16,24},{1,9},{9,17},{17,25},{2,10},{10,18},{18,26},{... | collective-permute-start | bytes 2359304 | tf_op jit(solution)/shard_map/ppermute | solution.py:30
  155.5 8.7 %copy-start.2 = (f32[8,12,96,128]{3,2,1,0:T(8,128)}, f32[8,12,96,128]{3,2,1,0:T(8,128)S(1)}, u32[]{:S(2)}) copy-start(f32[8,12,96,128]{3,2,1,0:T(8,128)S(1)} %fusion.1) | copy-start | bytes 14155780
  155.6 7.4 %collective-permute-start.3 = (f32[8,12,2,128]{3,2,1,0:T(2,128)S(1)}, f32[8,12,2,128]{3,2,1,0:T(2,128)S(1)}, u32[]{:S(2)}, u32[]{:S(2)}) collective-permute-start(f32[8,12,2,128]{3,2,1,0:T(2,128)S(1)} %get-tuple-element.14), channel_id=1, source_target_pairs={{0,1},{1,2},{2,3},{3,4},{4,5},{5,6},{6,7},{7,0},{8,9},{9,10},{10,1... | collective-permute-start | bytes 294920 | tf_op jit(solution)/shard_map/ppermute | solution.py:30
  157.6 6.5 %collective-permute-start.4 = (f32[8,12,2,128]{3,2,1,0:T(2,128)S(1)}, f32[8,12,2,128]{3,2,1,0:T(2,128)S(1)}, u32[]{:S(2)}, u32[]{:S(2)}) collective-permute-start(f32[8,12,2,128]{3,2,1,0:T(2,128)S(1)} %get-tuple-element.15), channel_id=1, source_target_pairs={{1,0},{2,1},{3,2},{4,3},{5,4},{6,5},{7,6},{0,7},{9,8},{10,9},{11,1... | collective-permute-start | bytes 294920 | tf_op jit(solution)/shard_map/ppermute | solution.py:32
  174.3 6.9 %slice-start = ((s8[4718592]{0:T(1024)(128)(4,1)}), s8[524288]{0:T(1024)(128)(4,1)S(1)}, s32[]{:S(2)}) async-start(s8[4718592]{0:T(1024)(128)(4,1)} %bitcast.60), calls=%async_computation.2 | async-start | bytes 1048576
  178.3 3.0 %slice-start.1 = ((s8[4718592]{0:T(1024)(128)(4,1)}), s8[4194304]{0:T(1024)(128)(4,1)S(1)}, s32[]{:S(2)}) async-start(s8[4718592]{0:T(1024)(128)(4,1)} %bitcast.60), calls=%async_computation.3 | async-start | bytes 8388608
  202.9 1.8 copy-start.1
where the time goes:
time: 205 us
  waiting for transfers between devices  123 us (60%)
  local copies, waits for them, and re-layouts  30.1 us (15%)
  other arithmetic  27.1 us (13%)
  starting transfers between devices  20.8 us (10%)
  matrix products  2.94 us (1%)
    ppermute x1, waiting for transfers between devices, shifted_2(): return lax.ppermute(block, axis, route)  47.9 us
    all_to_all x1, waiting for transfers between devices, local(): lax.all_to_all(filtered, 'phi', split_axis=1, concat_axis=0, tiled=True)  36.6 us
    all_to_all x1, waiting for transfers between devices, local(): lax.all_to_all(slot_rows, 'phi', split_axis=0, concat_axis=1, tiled=True)  34.4 us
    slice x3, local copies, waits for them, and re-layouts, local(): padded = jnp.pad(wrapped, ((0, 0), (0, 0), (0, 0), (2, 2)), mode='edge')  13.3 us
    concatenate x1, other arithmetic, local(): padded = jnp.pad(wrapped, ((0, 0), (0, 0), (0, 0), (2, 2)), mode='edge')  8.38 us
    all_to_all x1, starting transfers between devices, local(): lax.all_to_all(slot_rows, 'phi', split_axis=0, concat_axis=1, tiled=True)  7.25 us
    ppermute x2, starting transfers between devices, with_halo(): lax.ppermute(tail, axis, [(i, (i + 1) % count) for i in range(ends)])  5.14 us
    squeeze x1, local copies, waits for them, and re-layouts, advance(): extended[5 + component]  4.6 us
  transfers between devices with their start and end apart: 7, of which 5 were waited for; matrix products, arithmetic and copies ran while one was open for 1% of the time, Pallas kernels for 0%

commit v1 on v0

v1 whole, which is shorter than its diff:
```python
import functools
import math

import jax
import jax.numpy as jnp
import numpy as np
import ml_dtypes
from jax import lax
from jax.experimental import pallas as pl
from jax.experimental.pallas import tpu as pltpu
from jax.sharding import PartitionSpec as P

CAP = 4
KMAX = 128
TIME_STEP = 0.2
CHANNELS = 8
ODD = (3, 4, 6, 7)
BTHETA = 6
BPHI = 7
MESH = pl.DeviceIdType.MESH


def split_table(table):
    high = table.astype(ml_dtypes.bfloat16)
    low = (table - high.astype(np.float64)).astype(ml_dtypes.bfloat16)
    return np.stack([high, low])


def tables(count, cols):
    cycle = count * cols
    orders = np.arange(KMAX)
    points = np.arange(cycle)
    angle = (orders[:, None] * points[None, :] % cycle) * (2.0 * math.pi / cycle)
    forward = np.concatenate([np.cos(angle), np.sin(angle)], axis=0)
    offset = np.concatenate([np.arange(cols + 7), [-1]])
    place = ((np.arange(count)[:, None] * cols + offset[None, :]) % cycle).reshape(-1)
    back = forward.T[place]
    return split_table(forward), split_table(back)


def flux(ql, qr, vl, vr):
    return 0.5 * (ql * vl + qr * vr) - 0.5 * jnp.maximum(jnp.abs(vl), jnp.abs(vr)) * (qr - ql)


def stencil_row(ext, dout, bout, row, rows, cols):
    wide = cols + 8
    lower = jnp.where(row == 0, rows + 2, row - 1)
    upper = row + 1
    upper2 = row + 2
    lane = lax.broadcasted_iota(jnp.int32, (wide, 128), 1)
    first = lane == 0
    last = lane == 127

    def from_left(x):
        return pltpu.roll(x, 1, 0)

    def from_right(x):
        return pltpu.roll(x, wide - 1, 0)

    def from_below(x):
        return pltpu.roll(x, 1, 1)

    def from_above(x):
        return pltpu.roll(x, 127, 1)

    vr, vt, vp = ext[2, row], ext[3, row], ext[4, row]
    vt_lo, vt_up = ext[3, lower], ext[3, upper]
    vp_l = from_left(vp)
    vr_b = jnp.where(first, vr, from_below(vr))
    for c in range(2):
        q = ext[c, row]
        tend = flux(q, ext[c, upper], vt, vt_up) - flux(ext[c, lower], q, vt_lo, vt)
        fp = flux(from_left(q), q, vp_l, vp)
        tend = tend + from_right(fp) - fp
        fr = flux(jnp.where(first, q, from_below(q)), q, vr_b, vr)
        tend = tend + jnp.where(last, q * vr, from_above(fr)) - fr
        new = q - TIME_STEP * tend
        dout[c, row] = new[:cols]

    def emfs(j, bt_next):
        ur, ut, up = ext[2, j], ext[3, j], ext[4, j]
        br, bt, bp = ext[5, j], ext[6, j], ext[7, j]
        br_c = 0.5 * (br + jnp.where(last, br, from_above(br)))
        bt_c = 0.5 * (bt + bt_next)
        bp_c = 0.5 * (bp + from_right(bp))
        e_r = -(ut * bp_c - up * bt_c)
        e_p = -(ur * bt_c - ut * br_c)
        e_p0 = -(ur * bt_c - ut * br)
        pair_p = e_p + jnp.where(first, e_p0, from_below(e_p))
        pair_r = e_r + from_left(e_r)
        return e_p, pair_p, pair_r, br_c, bp_c

    bt = ext[6, row]
    bt_up = ext[6, upper]
    ep_lo, pp_lo, pr_lo, _, _ = emfs(lower, bt)
    ep, pp, pr, br_c, bp_c = emfs(row, bt_up)
    ep_up, pp_up, pr_up, _, _ = emfs(upper, ext[6, upper2])
    br = ext[5, row]
    e_t = -(vp * br_c - vr * bp_c)
    e_t0 = -(vp * br - vr * bp_c)
    et_pair = e_t + from_left(e_t)
    et_pair0 = e_t0 + from_left(e_t0)
    edge_t = et_pair + jnp.where(first, et_pair0, from_below(et_pair))
    edge_t_above = jnp.where(last, 2.0 * et_pair, from_above(edge_t))
    edge_p = pp_lo + pp
    edge_p_above = jnp.where(last, 2.0 * (ep_lo + ep), from_above(edge_p))
    edge_r = pr_lo + pr
    scale = TIME_STEP * 0.25
    new_r = br - scale * ((pp_up - pp_lo) - (from_right(edge_t) - edge_t))
    new_t = bt - scale * ((from_right(edge_r) - edge_r) - (edge_p_above - edge_p))
    new_p = ext[7, row] - scale * ((edge_t_above - edge_t) - (pr_up - pr_lo))
    bout[0, row] = new_r[:cols]
    bout[1, row] = new_t[:cols]
    bout[2, row] = new_p[:cols]


def split(x):
    high = x.astype(jnp.bfloat16)
    return high, (x - high.astype(jnp.float32)).astype(jnp.bfloat16)


def product(table, x):
    high, low = split(x)
    dot = functools.partial(jnp.dot, preferred_element_type=jnp.float32)
    return dot(table[0], high) + (dot(table[0], low) + dot(table[1], high))


def kernel(
    n, nt, rows, cols,
    density, velocity, bfield, levels, fwd_hbm, back_hbm,
    dout, bout,
    ext, cyc, fil, caps, fwd, back, to_right, to_left, at_left, at_right,
    load_sem, fs, fr, rs, rr, gs, gr, g2s, g2r, hs, hr, ts, tr,
):
    per = CHANNELS * CAP // n
    groups = per // 2
    wide = cols + 8
    cycle = n * cols
    t = lax.axis_index("theta")
    me = lax.axis_index("phi")
    north = t == 0
    south = t == nt - 1
    end = north | south
    cap0 = jnp.where(north, 0, rows - CAP)
    main = pl.ds(0, cols)

    loads = [
        pltpu.make_async_copy(density, ext.at[pl.ds(0, 2), pl.ds(0, rows), main], load_sem.at[0]),
        pltpu.make_async_copy(velocity, ext.at[pl.ds(2, 3), pl.ds(0, rows), main], load_sem.at[1]),
        pltpu.make_async_copy(bfield, ext.at[pl.ds(5, 3), pl.ds(0, rows), main], load_sem.at[2]),
    ]
    table_loads = [
        pltpu.make_async_copy(fwd_hbm, fwd, load_sem.at[3]),
        pltpu.make_async_copy(back_hbm, back, load_sem.at[4]),
    ]
    for copy in loads + table_loads:
        copy.start()

    barrier = pltpu.get_barrier_semaphore()

    def other(d):
        return lax.rem(me + d, n)

    def greet(device):
        pl.semaphore_signal(barrier, inc=1, device_id=device, device_id_type=MESH)

    right, left = other(1), other(n - 1)

    @pl.when(end)
    def _():
        for d in range(1, n):
            greet({"phi": other(d)})

    @pl.when(jnp.logical_not(end))
    def _():
        greet({"phi": right})
        greet({"phi": left})

    @pl.when(t > 0)
    def _():
        greet({"theta": t - 1})

    @pl.when(t < nt - 1)
    def _():
        greet({"theta": t + 1})

    @pl.when(end)
    def _():
        pl.semaphore_wait(barrier, n)

    @pl.when(jnp.logical_not(end))
    def _():
        pl.semaphore_wait(barrier, 4)

    for copy in loads:
        copy.wait()

    def slot_place(owner, g):
        slot = owner * per + 2 * g
        return lax.div(slot, CAP), cap0 + lax.rem(slot, CAP)

    def remote(src, dst, send, recv, device):
        return pltpu.make_async_remote_copy(
            src_ref=src, dst_ref=dst, send_sem=send, recv_sem=recv,
            device_id=device, device_id_type=MESH,
        )

    def forward_copy(g, d):
        q = other(d)
        ch, r = slot_place(q, g)
        src = ext.at[ch, pl.ds(r, 2), main]
        dst = cyc.at[pl.ds(2 * g, 2), pl.ds(pl.multiple_of(me * cols, 8), cols)]
        if d == 0:
            return pltpu.make_async_copy(src, dst, fr.at[g, 0])
        return remote(src, dst, fs.at[g, d], fr.at[g, d], {"phi": q})

    def return_copy(g, d):
        q = other(d)
        src = fil.at[pl.ds(2 * g, 2), q]
        dst = caps.at[pl.ds(me * per + 2 * g, 2)]
        if d == 0:
            return pltpu.make_async_copy(src, dst, rr.at[g, 0])
        return remote(src, dst, rs.at[g, d], rr.at[g, d], {"phi": q})

    def ghost_copy(slot, channel, ghost_row, d, send, recv):
        q = other(d)
        src = fil.at[slot, other(d + n // 2)]
        dst = ext.at[channel, ghost_row]
        if d == 0:
            return pltpu.make_async_copy(src, dst, recv.at[0])
        return remote(src, dst, send.at[d], recv.at[d], {"phi": q})

    for c in range(CHANNELS):
        to_right[c] = ext[c, 0:rows, cols - 1]
        to_left[c] = ext[c, 0:rows, 0]
    to_left[CHANNELS] = ext[BPHI, 0:rows, 1]

    @pl.when(end)
    def _():
        for g in range(groups):
            for d in range(n):
                forward_copy(g, d).start()

    go_right = remote(to_right, at_left, hs.at[0], hr.at[0], {"phi": right})
    go_left = remote(to_left, at_right, hs.at[1], hr.at[1], {"phi": left})
    go_right.start()
    go_left.start()
    go_right.wait()
    go_left.wait()

    def unpack(lo, hi):
        for c in range(CHANNELS):
            ext[c, lo:hi, wide - 1] = at_left[c, lo:hi]
            ext[c, lo:hi, cols] = at_right[c, lo:hi]
        ext[BPHI, lo:hi, cols + 1] = at_right[CHANNELS, lo:hi]

    @pl.when(north)
    def _():
        unpack(CAP, rows)

    @pl.when(south)
    def _():
        unpack(0, rows - CAP)

    @pl.when(jnp.logical_not(end))
    def _():
        unpack(0, rows)

    every = pl.ds(0, CHANNELS)
    down = remote(ext.at[every, rows - 1], ext.at[every, rows + 2], ts.at[0], tr.at[0], {"theta": t + 1})
    up = remote(ext.at[every, 0], ext.at[every, rows], ts.at[1], tr.at[1], {"theta": t - 1})
    up2 = remote(ext.at[BTHETA, 1], ext.at[BTHETA, rows + 1], ts.at[2], tr.at[2], {"theta": t - 1})

    @pl.when(t < nt - 1)
    def _():
        down.start()

    @pl.when(t > 0)
    def _():
        up.start()
        up2.start()

    @pl.when(t > 0)
    def _():
        down.wait_recv()

    @pl.when(t < nt - 1)
    def _():
        up.wait_recv()
        up2.wait_recv()

    def sweep(lo, hi):
        def body(row, carry):
            stencil_row(ext, dout, bout, row, rows, cols)
            return carry

        lax.fori_loop(lo, hi, body, 0)

    early_lo = jnp.where(north, CAP + 1, 0)
    early_hi = jnp.where(south, rows - CAP - 2, rows)
    sweep(early_lo, early_hi)
    for copy in table_loads:
        copy.wait()

    @pl.when(end)
    def _():
        pole = jnp.where(north, 0, 1)
        mode = lax.rem(lax.broadcasted_iota(jnp.int32, (2 * KMAX, 128), 0), KMAX)
        weight = jnp.where(mode == 0, 1.0 / cycle, 2.0 / cycle)
        for g in range(groups):
            for d in range(n):
                copy = forward_copy(g, d)
                copy.wait() if d == 0 else copy.wait_recv()
            masks = []
            for s in (2 * g, 2 * g + 1):
                limit = lax.shift_right_logical(jnp.int32(KMAX), levels[pole, lax.rem(me * per + s, CAP)])
                masks.append(jnp.where(mode < limit, weight, 0.0))
            both = jnp.concatenate([cyc[2 * g], cyc[2 * g + 1]], axis=1)
            coeffs = product(fwd, both) * jnp.concatenate(masks, axis=1)
            values = product(back, coeffs)
            fil[2 * g] = values[:, :128].reshape(n, wide, 128)
            fil[2 * g + 1] = values[:, 128:].reshape(n, wide, 128)
            for d in range(n):
                return_copy(g, d).start()

    south_slot = per - 1
    second = BTHETA * CAP + CAP - 2
    second_owner, second_slot = second // per, second % per

    def north_ghost(owner, d):
        return ghost_copy(0, lax.div(owner * per, CAP), rows + 2, d, gs, gr)

    def south_ghost(owner, d):
        return ghost_copy(south_slot, lax.div(owner * per, CAP), rows, d, gs, gr)

    def second_ghost(d):
        return ghost_copy(second_slot, BTHETA, rows + 1, d, g2s, g2r)

    def has_first(owner):
        return lax.rem(owner * per, CAP) == 0

    def has_last(owner):
        return lax.rem(owner * per + per - 1, CAP) == CAP - 1

    @pl.when(north & has_first(me))
    def _():
        for d in range(n):
            north_ghost(me, d).start()

    @pl.when(south & has_last(me))
    def _():
        for d in range(n):
            south_ghost(me, d).start()

    @pl.when(south & (me == second_owner))
    def _():
        for d in range(n):
            second_ghost(d).start()

    @pl.when(end)
    def _():
        for g in range(groups):
            for d in range(1, n):
                forward_copy(g, d).wait_send()
            for d in range(n):
                copy = return_copy(g, d)
                copy.wait() if d == 0 else copy.wait_recv()

        def place(slot, carry):
            ext[lax.div(slot, CAP), cap0 + lax.rem(slot, CAP)] = caps[slot]
            return carry

        lax.fori_loop(0, CHANNELS * CAP, place, 0)

    for d in range(n):
        source = other(n - d)

        @pl.when(north & has_first(source))
        def _():
            copy = north_ghost(source, d)
            copy.wait() if d == 0 else copy.wait_recv()

        @pl.when(south & has_last(source))
        def _():
            copy = south_ghost(source, d)
            copy.wait() if d == 0 else copy.wait_recv()

        @pl.when(south & (source == second_owner))
        def _():
            copy = second_ghost(d)
            copy.wait() if d == 0 else copy.wait_recv()

    @pl.when(north)
    def _():
        for c in ODD:
            ext[c, rows + 2] = -ext[c, rows + 2]

    @pl.when(south)
    def _():
        for c in ODD:
            ext[c, rows] = -ext[c, rows]
        ext[BTHETA, rows + 1] = -ext[BTHETA, rows + 1]

    late_lo = jnp.where(south, rows - CAP - 2, 0)
    late_hi = jnp.where(north, CAP + 1, jnp.where(south, rows, 0))
    sweep(late_lo, late_hi)

    @pl.when(t < nt - 1)
    def _():
        down.wait_send()

    @pl.when(t > 0)
    def _():
        up.wait_send()
        up2.wait_send()

    @pl.when(end)
    def _():
        for g in range(groups):
            for d in range(1, n):
                return_copy(g, d).wait_send()

    @pl.when(north & has_first(me))
    def _():
        for d in range(1, n):
            north_ghost(me, d).wait_send()

    @pl.when(south & has_last(me))
    def _():
        for d in range(1, n):
            south_ghost(me, d).wait_send()

    @pl.when(south & (me == second_owner))
    def _():
        for d in range(1, n):
            second_ghost(d).wait_send()


def local(n, nt, density, velocity, bfield, levels):
    _, rows, cols, radial = density.shape
    per = CHANNELS * CAP // n
    groups = per // 2
    wide = cols + 8
    forward, back = tables(n, cols)
    any_space = pl.BlockSpec(memory_space=pl.ANY)
    vmem = pl.BlockSpec(memory_space=pltpu.VMEM)
    f32 = jnp.float32
    dma = pltpu.SemaphoreType.DMA
    return pl.pallas_call(
        functools.partial(kernel, n, nt, rows, cols),
        out_shape=(
            jax.ShapeDtypeStruct(density.shape, f32),
            jax.ShapeDtypeStruct(bfield.shape, f32),
        ),
        in_specs=[any_space] * 3 + [pl.BlockSpec(memory_space=pltpu.SMEM)] + [any_space] * 2,
        out_specs=(vmem, vmem),
        scratch_shapes=[
            pltpu.VMEM((CHANNELS, rows + 3, wide, radial), f32),
            pltpu.VMEM((per, n * cols, radial), f32),
            pltpu.VMEM((per, n, wide, radial), f32),
            pltpu.VMEM((CHANNELS * CAP, wide, radial), f32),
            pltpu.VMEM(forward.shape, jnp.bfloat16),
            pltpu.VMEM(back.shape, jnp.bfloat16),
            pltpu.VMEM((CHANNELS, rows, radial), f32),
            pltpu.VMEM((CHANNELS + 1, rows, radial), f32),
            pltpu.VMEM((CHANNELS, rows, radial), f32),
            pltpu.VMEM((CHANNELS + 1, rows, radial), f32),
            dma((5,)),
            dma((groups, n)),
            dma((groups, n)),
            dma((groups, n)),
            dma((groups, n)),
            dma((n,)),
            dma((n,)),
            dma((n,)),
            dma((n,)),
            dma((2,)),
            dma((2,)),
            dma((3,)),
            dma((3,)),
        ],
        compiler_params=pltpu.CompilerParams(
            collective_id=0, has_side_effects=True, vmem_limit_bytes=40 * 1024 * 1024
        ),
        name="substep",
    )(density, velocity, bfield, levels, jnp.asarray(forward), jnp.asarray(back))


def solution(mesh):
    spec = P(None, "theta", "phi", None)
    return jax.shard_map(
        functools.partial(local, mesh.shape["phi"], mesh.shape["theta"]),
        mesh=mesh,
        in_specs=(spec, spec, spec, P()),
        out_specs=(spec, spec),
        check_vma=False,
    )
```

time: 205 us -> 63.5 us (0.31)
  waiting for transfers between devices: 123 us -> 0 us
  Pallas kernels: 0 us -> 53.7 us
  other arithmetic: 27.1 us -> 0 us
  local copies, waits for them, and re-layouts: 30.1 us -> 8.53 us
  starting transfers between devices: 20.8 us -> 0 us
  matrix products: 2.94 us -> 0 us
    all_to_all x2 -> x0, waiting for transfers between devices: 71 us -> none  [the longest x1 36.6 us: local(): lax.all_to_all(filtered, 'phi', split_axis=1, concat_axis=0, tiled=True)]
    pallas_call x0 -> x1, Pallas kernels: none -> 53.7 us  [local(): pl.pallas_call(functools.partial(kernel, n, nt, rows, cols), out_shape=(j...]
    ppermute x5 -> x0, waiting for transfers between devices: 51.7 us -> none  [the longest x1 47.9 us: shifted_2(): return lax.ppermute(block, axis, route)]
    slice x6 -> x0, local copies, waits for them, and re-layouts: 13.5 us -> none  [the longest x3 13.3 us: local(): padded = jnp.pad(wrapped, ((0, 0), (0, 0), (0, 0), (2, 2)), mode='edge')]
    all_to_all x2 -> x0, starting transfers between devices: 11.6 us -> none  [the longest x1 7.25 us: local(): lax.all_to_all(slot_rows, 'phi', split_axis=0, concat_axis=1, tiled=True)]
    concatenate x3 -> x0, other arithmetic: 9.27 us -> none  [the longest x1 8.38 us: local(): padded = jnp.pad(wrapped, ((0, 0), (0, 0), (0, 0), (2, 2)), mode='edge')]
    ppermute x5 -> x0, starting transfers between devices: 9.22 us -> none  [the longest x2 5.14 us: with_halo(): lax.ppermute(tail, axis, [(i, (i + 1) % count) for i in range(ends)])]
    unnamed x22 -> x14, local copies, waits for them, and re-layouts: 3.45 us -> 8.53 us
  transfers between devices with their start and end apart: 7 -> 0, of which waited for: 5 -> 0; matrix products, arithmetic and copies ran while one was open for 1% -> 0% of each run, Pallas kernels for 0% -> 0%
where the time goes in v1:
time: 63.5 us; the launch traced here: 62.8 us
  Pallas kernels  53.7 us (85%)
  local copies, waits for them, and re-layouts  8.53 us (13%)
  between operations  0.65 us (1%)
    pallas_call x1, Pallas kernels, local(): pl.pallas_call(functools.partial(kernel, n, nt, rows, cols), out_shape=(j...  53.7 us
    unnamed x14, local copies, waits for them, and re-layouts  8.53 us

profile of v1, /device:TPU:0, one launch (start us, length us, event | category | flops | bytes accessed | tf_op | source)
XLA Modules:
  0.0 62.8 jit_solution(12530134936672819599)
XLA Ops:
  0.6 0.0 copy-start
  0.6 1.3 %copy-done = f32[3,8,96,128]{3,2,1,0:T(8,128)S(1)} copy-done((f32[3,8,96,128]{3,2,1,0:T(8,128)S(1)}, f32[3,8,96,128]{3,2,1,0:T(8,128)}, u32[]{:S(2)}) %copy-start) | copy-done | bytes 1179672
  1.9 0.0 copy-start.1
  1.9 1.3 %copy-done.1 = f32[3,8,96,128]{3,2,1,0:T(8,128)S(1)} copy-done((f32[3,8,96,128]{3,2,1,0:T(8,128)S(1)}, f32[3,8,96,128]{3,2,1,0:T(8,128)}, u32[]{:S(2)}) %copy-start.1) | copy-done | bytes 1179672
  3.2 0.0 copy-start.2
  3.2 1.2 %copy-done.2 = bf16[2,832,256]{2,1,0:T(8,128)(2,1)S(1)} copy-done((bf16[2,832,256]{2,1,0:T(8,128)(2,1)S(1)}, bf16[2,832,256]{2,1,0:T(8,128)(2,1)}, u32[]{:S(2)}) %copy-start.2) | copy-done | bytes 851992
  4.3 0.0 copy-start.3
  4.3 1.1 %copy-done.3 = f32[2,8,96,128]{3,2,1,0:T(8,128)S(1)} copy-done((f32[2,8,96,128]{3,2,1,0:T(8,128)S(1)}, f32[2,8,96,128]{3,2,1,0:T(8,128)}, u32[]{:S(2)}) %copy-start.3) | copy-done | bytes 786456
  5.5 0.0 copy-start.4
  5.5 1.1 %copy-done.4 = bf16[2,256,768]{2,1,0:T(8,128)(2,1)S(1)} copy-done((bf16[2,256,768]{2,1,0:T(8,128)(2,1)S(1)}, bf16[2,256,768]{2,1,0:T(8,128)(2,1)}, u32[]{:S(2)}) %copy-start.4) | copy-done | bytes 786456
  6.6 0.0 copy-start.5
  6.6 0.7 %copy-done.5 = s32[2,4]{1,0:T(2,128)S(1)} copy-done((s32[2,4]{1,0:T(2,128)S(1)}, s32[2,4]{1,0:T(2,128)}, u32[]{:S(2)}) %copy-start.5) | copy-done | bytes 56
  7.3 53.7 %substep.1 = (f32[2,8,96,128]{3,2,1,0:T(8,128)S(1)}, f32[3,8,96,128]{3,2,1,0:T(8,128)S(1)}) custom-call(f32[2,8,96,128]{3,2,1,0:T(8,128)S(1)} %copy-done.3, f32[3,8,96,128]{3,2,1,0:T(8,128)S(1)} %copy-done, f32[3,8,96,128]{3,2,1,0:T(8,128)S(1)} %copy-done.1, s32[2,4]{1,0:T(2,128)S(1)} %copy-done.5, bf16[2,256,768]{2,1,0:T(8,128)(2,1)S(1)} %copy-done.4, ...), custom_call_target="tpu_custom_call" | custom-call | tf_op jit(solution)/shard_map/substep/pallas_call | solution.py:449
  60.9 0.9 %copy.10 = f32[2,8,96,128]{3,2,1,0:T(8,128)} copy(f32[2,8,96,128]{3,2,1,0:T(8,128)S(1)} %get-tuple-element.4) | data formatting | bytes 1572864
  61.8 1.0 %copy.11 = f32[3,8,96,128]{3,2,1,0:T(8,128)} copy(f32[3,8,96,128]{3,2,1,0:T(8,128)S(1)} %get-tuple-element.5) | data formatting | bytes 2359296
Async XLA Ops:
  0.6 1.3 %copy-start = (f32[3,8,96,128]{3,2,1,0:T(8,128)S(1)}, f32[3,8,96,128]{3,2,1,0:T(8,128)}, u32[]{:S(2)}) copy-start(f32[3,8,96,128]{3,2,1,0:T(8,128)} %velocity.1) | copy-start | bytes 3538948
  1.9 1.3 %copy-start.1 = (f32[3,8,96,128]{3,2,1,0:T(8,128)S(1)}, f32[3,8,96,128]{3,2,1,0:T(8,128)}, u32[]{:S(2)}) copy-start(f32[3,8,96,128]{3,2,1,0:T(8,128)} %bfield.1) | copy-start | bytes 3538948
  3.2 1.2 %copy-start.2 = (bf16[2,832,256]{2,1,0:T(8,128)(2,1)S(1)}, bf16[2,832,256]{2,1,0:T(8,128)(2,1)}, u32[]{:S(2)}) copy-start(bf16[2,832,256]{2,1,0:T(8,128)(2,1)} %constant.5.clone.back_hbm) | copy-start | bytes 2555908
  4.3 1.1 %copy-start.3 = (f32[2,8,96,128]{3,2,1,0:T(8,128)S(1)}, f32[2,8,96,128]{3,2,1,0:T(8,128)}, u32[]{:S(2)}) copy-start(f32[2,8,96,128]{3,2,1,0:T(8,128)} %density.1) | copy-start | bytes 2359300
  5.5 1.1 %copy-start.4 = (bf16[2,256,768]{2,1,0:T(8,128)(2,1)S(1)}, bf16[2,256,768]{2,1,0:T(8,128)(2,1)}, u32[]{:S(2)}) copy-start(bf16[2,256,768]{2,1,0:T(8,128)(2,1)} %constant.4.clone.fwd_hbm) | copy-start | bytes 2359300
  6.6 0.7 %copy-start.5 = (s32[2,4]{1,0:T(2,128)S(1)}, s32[2,4]{1,0:T(2,128)}, u32[]{:S(2)}) copy-start(s32[2,4]{1,0:T(2,128)} %levels.1) | copy-start | bytes 100

commit v2 on v1

--- a/solution.py
+++ b/solution.py
@@ -195,9 +195,13 @@
     for copy in loads:
         copy.wait()
 
+    def cap_row(slot):
+        row = lax.rem(slot, CAP)
+        return jnp.where(north, CAP - 2 - row, row)
+
     def slot_place(owner, g):
         slot = owner * per + 2 * g
-        return lax.div(slot, CAP), cap0 + lax.rem(slot, CAP)
+        return lax.div(slot, CAP), cap0 + cap_row(slot)
 
     def remote(src, dst, send, recv, device):
         return pltpu.make_async_remote_copy(
@@ -230,21 +234,24 @@
             return pltpu.make_async_copy(src, dst, recv.at[0])
         return remote(src, dst, send.at[d], recv.at[d], {"phi": q})
 
+    far_first = sorted(range(n), key=lambda d: -min(d, n - d))
+
     for c in range(CHANNELS):
         to_right[c] = ext[c, 0:rows, cols - 1]
         to_left[c] = ext[c, 0:rows, 0]
     to_left[CHANNELS] = ext[BPHI, 0:rows, 1]
 
-    @pl.when(end)
-    def _():
-        for g in range(groups):
-            for d in range(n):
-                forward_copy(g, d).start()
-
     go_right = remote(to_right, at_left, hs.at[0], hr.at[0], {"phi": right})
     go_left = remote(to_left, at_right, hs.at[1], hr.at[1], {"phi": left})
     go_right.start()
     go_left.start()
+
+    @pl.when(end)
+    def _():
+        for g in range(groups):
+            for d in far_first:
+                forward_copy(g, d).start()
+
     go_right.wait()
     go_left.wait()
 
@@ -313,22 +320,23 @@
                 copy.wait() if d == 0 else copy.wait_recv()
             masks = []
             for s in (2 * g, 2 * g + 1):
-                limit = lax.shift_right_logical(jnp.int32(KMAX), levels[pole, lax.rem(me * per + s, CAP)])
+                limit = lax.shift_right_logical(jnp.int32(KMAX), levels[pole, cap_row(me * per + 2 * g) + s - 2 * g])
                 masks.append(jnp.where(mode < limit, weight, 0.0))
             both = jnp.concatenate([cyc[2 * g], cyc[2 * g + 1]], axis=1)
             coeffs = product(fwd, both) * jnp.concatenate(masks, axis=1)
             values = product(back, coeffs)
             fil[2 * g] = values[:, :128].reshape(n, wide, 128)
             fil[2 * g + 1] = values[:, 128:].reshape(n, wide, 128)
-            for d in range(n):
+            for d in far_first:
                 return_copy(g, d).start()
 
+    north_slot = per - 2
     south_slot = per - 1
     second = BTHETA * CAP + CAP - 2
     second_owner, second_slot = second // per, second % per
 
     def north_ghost(owner, d):
-        return ghost_copy(0, lax.div(owner * per, CAP), rows + 2, d, gs, gr)
+        return ghost_copy(north_slot, lax.div(owner * per, CAP), rows + 2, d, gs, gr)
 
     def south_ghost(owner, d):
         return ghost_copy(south_slot, lax.div(owner * per, CAP), rows, d, gs, gr)
@@ -336,18 +344,15 @@
     def second_ghost(d):
         return ghost_copy(second_slot, BTHETA, rows + 1, d, g2s, g2r)
 
-    def has_first(owner):
-        return lax.rem(owner * per, CAP) == 0
-
-    def has_last(owner):
-        return lax.rem(owner * per + per - 1, CAP) == CAP - 1
-
-    @pl.when(north & has_first(me))
+    def has_edge(owner):
+        return lax.rem(owner * per + per, CAP) == 0
+
+    @pl.when(north & has_edge(me))
     def _():
         for d in range(n):
             north_ghost(me, d).start()
 
-    @pl.when(south & has_last(me))
+    @pl.when(south & has_edge(me))
     def _():
         for d in range(n):
             south_ghost(me, d).start()
@@ -362,25 +367,37 @@
         for g in range(groups):
             for d in range(1, n):
                 forward_copy(g, d).wait_send()
-            for d in range(n):
-                copy = return_copy(g, d)
-                copy.wait() if d == 0 else copy.wait_recv()
-
-        def place(slot, carry):
-            ext[lax.div(slot, CAP), cap0 + lax.rem(slot, CAP)] = caps[slot]
+
+    def take(g):
+        for d in range(n):
+            copy = return_copy(g, d)
+            copy.wait() if d == 0 else copy.wait_recv()
+
+        def place(owner, carry):
+            ch, r = slot_place(owner, g)
+            ext[ch, r] = caps[owner * per + 2 * g]
+            ext[ch, r + 1] = caps[owner * per + 2 * g + 1]
             return carry
 
-        lax.fori_loop(0, CHANNELS * CAP, place, 0)
+        lax.fori_loop(0, n, place, 0)
+
+    for g in range(groups):
+
+        @pl.when(end)
+        def _():
+            take(g)
+            if groups == 2 and g == 0:
+                sweep(jnp.where(north, CAP - 1, rows - CAP - 2), jnp.where(north, CAP + 1, rows - CAP))
 
     for d in range(n):
         source = other(n - d)
 
-        @pl.when(north & has_first(source))
+        @pl.when(north & has_edge(source))
         def _():
             copy = north_ghost(source, d)
             copy.wait() if d == 0 else copy.wait_recv()
 
-        @pl.when(south & has_last(source))
+        @pl.when(south & has_edge(source))
         def _():
             copy = south_ghost(source, d)
             copy.wait() if d == 0 else copy.wait_recv()
@@ -401,8 +418,8 @@
             ext[c, rows] = -ext[c, rows]
         ext[BTHETA, rows + 1] = -ext[BTHETA, rows + 1]
 
-    late_lo = jnp.where(south, rows - CAP - 2, 0)
-    late_hi = jnp.where(north, CAP + 1, jnp.where(south, rows, 0))
+    late_lo = jnp.where(south, rows - CAP - 2 if groups != 2 else rows - CAP, 0)
+    late_hi = jnp.where(north, CAP + 1 if groups != 2 else CAP - 1, jnp.where(south, rows, 0))
     sweep(late_lo, late_hi)
 
     @pl.when(t < nt - 1)
@@ -420,12 +437,12 @@
             for d in range(1, n):
                 return_copy(g, d).wait_send()
 
-    @pl.when(north & has_first(me))
+    @pl.when(north & has_edge(me))
     def _():
         for d in range(1, n):
             north_ghost(me, d).wait_send()
 
-    @pl.when(south & has_last(me))
+    @pl.when(south & has_edge(me))
     def _():
         for d in range(1, n):
             south_ghost(me, d).wait_send()
@@ -480,7 +497,7 @@
             dma((3,)),
         ],
         compiler_params=pltpu.CompilerParams(
-            collective_id=0, has_side_effects=True, vmem_limit_bytes=40 * 1024 * 1024
+            collective_id=0, has_side_effects=True, vmem_limit_bytes=60 * 1024 * 1024
         ),
         name="substep",
     )(density, velocity, bfield, levels, jnp.asarray(forward), jnp.asarray(back))

time: 63.5 us -> 56.3 us (0.89)
  local copies, waits for them, and re-layouts: 8.53 us -> 3.18 us
  Pallas kernels: 53.7 us -> 51.6 us
    unnamed x14 -> x4, local copies, waits for them, and re-layouts: 8.53 us -> 3.18 us
    pallas_call x1, Pallas kernels: 53.7 us -> 51.6 us  [local(): pl.pallas_call(functools.partial(kernel, n, nt, rows, cols), out_shape=(j...]
where the time goes in v2:
time: 56.3 us; the launch traced here: 55.4 us
  Pallas kernels  51.6 us (92%)
  local copies, waits for them, and re-layouts  3.18 us (6%)
  between operations  0.65 us (1%)
    pallas_call x1, Pallas kernels, local(): pl.pallas_call(functools.partial(kernel, n, nt, rows, cols), out_shape=(j...  51.6 us
    unnamed x4, local copies, waits for them, and re-layouts  3.18 us

profile of v2, /device:TPU:0, one launch (start us, length us, event | category | flops | bytes accessed | tf_op | source)
XLA Modules:
  0.0 55.4 jit_solution(12425689933311851860)
XLA Ops:
  0.6 51.6 %substep.1 = (f32[2,8,96,128]{3,2,1,0:T(8,128)}, f32[3,8,96,128]{3,2,1,0:T(8,128)}) custom-call(f32[2,8,96,128]{3,2,1,0:T(8,128)} %density.1, f32[3,8,96,128]{3,2,1,0:T(8,128)} %velocity.1, f32[3,8,96,128]{3,2,1,0:T(8,128)} %bfield.1, s32[2,4]{1,0:T(2,128)} %levels.1, bf16[2,256,768]{2,1,0:T(8,128)(2,1)} %constant.4.clone.fwd_hbm, ...), custom_call_target="tpu_custom_call" | custom-call | tf_op jit(solution)/shard_map/substep/pallas_call | solution.py:466
  52.2 0.0 copy-start
  52.2 2.2 %copy.10 = f32[2,8,96,128]{3,2,1,0:T(8,128)} copy(f32[2,8,96,128]{3,2,1,0:T(8,128)} %get-tuple-element.4) | data formatting | bytes 1572864
  54.4 0.0 copy-done
  54.4 1.0 %copy.11 = f32[3,8,96,128]{3,2,1,0:T(8,128)} copy(f32[3,8,96,128]{3,2,1,0:T(8,128)S(1)} %copy-done) | data formatting | bytes 2359296
Async XLA Ops:
  52.2 2.2 %copy-start = (f32[3,8,96,128]{3,2,1,0:T(8,128)S(1)}, f32[3,8,96,128]{3,2,1,0:T(8,128)}, u32[]{:S(2)}) copy-start(f32[3,8,96,128]{3,2,1,0:T(8,128)} %get-tuple-element.5) | copy-start | bytes 3538948

commit v3 on v1

v3 whole, which is shorter than its diff:
```python
import functools
import math

import jax
import jax.numpy as jnp
import numpy as np
import ml_dtypes
from jax import lax
from jax.experimental import pallas as pl
from jax.experimental.pallas import tpu as pltpu
from jax.sharding import PartitionSpec as P

CAP = 4
KMAX = 128
TIME_STEP = 0.2
CHANNELS = 8
HUBS = 2
ODD = (3, 4, 6, 7)
BTHETA = 6
BPHI = 7
MESH = pl.DeviceIdType.MESH


def split_table(table):
    high = table.astype(ml_dtypes.bfloat16)
    low = (table - high.astype(np.float64)).astype(ml_dtypes.bfloat16)
    return np.stack([high, low])


def tables(count, cols):
    cycle = count * cols
    orders = np.arange(KMAX)
    points = np.arange(cycle)
    angle = (orders[:, None] * points[None, :] % cycle) * (2.0 * math.pi / cycle)
    forward = np.concatenate([np.cos(angle), np.sin(angle)], axis=0)
    offset = np.concatenate([np.arange(cols + 7), [-1]])
    place = ((np.arange(count)[:, None] * cols + offset[None, :]) % cycle).reshape(-1)
    back = forward.T[place]
    return split_table(forward), split_table(back)


def flux(ql, qr, vl, vr):
    return 0.5 * (ql * vl + qr * vr) - 0.5 * jnp.maximum(jnp.abs(vl), jnp.abs(vr)) * (qr - ql)


def stencil_row(ext, dout, bout, row, rows, cols):
    wide = cols + 8
    lower = jnp.where(row == 0, rows + 2, row - 1)
    upper = row + 1
    upper2 = row + 2
    lane = lax.broadcasted_iota(jnp.int32, (wide, 128), 1)
    first = lane == 0
    last = lane == 127

    def from_left(x):
        return pltpu.roll(x, 1, 0)

    def from_right(x):
        return pltpu.roll(x, wide - 1, 0)

    def from_below(x):
        return pltpu.roll(x, 1, 1)

    def from_above(x):
        return pltpu.roll(x, 127, 1)

    vr, vt, vp = ext[2, row], ext[3, row], ext[4, row]
    vt_lo, vt_up = ext[3, lower], ext[3, upper]
    vp_l = from_left(vp)
    vr_b = jnp.where(first, vr, from_below(vr))
    for c in range(2):
        q = ext[c, row]
        tend = flux(q, ext[c, upper], vt, vt_up) - flux(ext[c, lower], q, vt_lo, vt)
        fp = flux(from_left(q), q, vp_l, vp)
        tend = tend + from_right(fp) - fp
        fr = flux(jnp.where(first, q, from_below(q)), q, vr_b, vr)
        tend = tend + jnp.where(last, q * vr, from_above(fr)) - fr
        new = q - TIME_STEP * tend
        dout[c, row] = new[:cols]

    def emfs(j, bt_next):
        ur, ut, up = ext[2, j], ext[3, j], ext[4, j]
        br, bt, bp = ext[5, j], ext[6, j], ext[7, j]
        br_c = 0.5 * (br + jnp.where(last, br, from_above(br)))
        bt_c = 0.5 * (bt + bt_next)
        bp_c = 0.5 * (bp + from_right(bp))
        e_r = -(ut * bp_c - up * bt_c)
        e_p = -(ur * bt_c - ut * br_c)
        e_p0 = -(ur * bt_c - ut * br)
        pair_p = e_p + jnp.where(first, e_p0, from_below(e_p))
        pair_r = e_r + from_left(e_r)
        return e_p, pair_p, pair_r, br_c, bp_c

    bt = ext[6, row]
    bt_up = ext[6, upper]
    ep_lo, pp_lo, pr_lo, _, _ = emfs(lower, bt)
    ep, pp, pr, br_c, bp_c = emfs(row, bt_up)
    ep_up, pp_up, pr_up, _, _ = emfs(upper, ext[6, upper2])
    br = ext[5, row]
    e_t = -(vp * br_c - vr * bp_c)
    e_t0 = -(vp * br - vr * bp_c)
    et_pair = e_t + from_left(e_t)
    et_pair0 = e_t0 + from_left(e_t0)
    edge_t = et_pair + jnp.where(first, et_pair0, from_below(et_pair))
    edge_t_above = jnp.where(last, 2.0 * et_pair, from_above(edge_t))
    edge_p = pp_lo + pp
    edge_p_above = jnp.where(last, 2.0 * (ep_lo + ep), from_above(edge_p))
    edge_r = pr_lo + pr
    scale = TIME_STEP * 0.25
    new_r = br - scale * ((pp_up - pp_lo) - (from_right(edge_t) - edge_t))
    new_t = bt - scale * ((from_right(edge_r) - edge_r) - (edge_p_above - edge_p))
    new_p = ext[7, row] - scale * ((edge_t_above - edge_t) - (pr_up - pr_lo))
    bout[0, row] = new_r[:cols]
    bout[1, row] = new_t[:cols]
    bout[2, row] = new_p[:cols]


def split(x):
    high = x.astype(jnp.bfloat16)
    return high, (x - high.astype(jnp.float32)).astype(jnp.bfloat16)


def product(table, x):
    high, low = split(x)
    dot = functools.partial(jnp.dot, preferred_element_type=jnp.float32)
    return dot(table[0], high) + (dot(table[0], low) + dot(table[1], high))


def kernel(
    n, nt, rows, cols,
    density, velocity, bfield, levels, fwd_hbm, back_hbm,
    dout, bout,
    ext, cyc, part, other_part, fil, gfil, caps, fwd, back, to_right, to_left, at_left, at_right,
    load_sem, fs, fr, ms, mr, rs, rr, gs, gr, g2s, g2r, hs, hr, ts, tr,
):
    half_n = n // 2
    groups = CHANNELS // HUBS * 2
    pole_groups = groups // 2
    wide = cols + 8
    cycle = n * cols
    t = lax.axis_index("theta")
    me = lax.axis_index("phi")
    north = t == 0
    south = t == nt - 1
    end = north | south
    cap0 = jnp.where(north, 0, rows - CAP)
    main = pl.ds(0, cols)
    half = lax.div(me, half_n)
    place = lax.rem(me, half_n)

    def hub_place(j):
        return jnp.where(half == 0, half_n - HUBS + j, j)

    hub_index = place - hub_place(0)
    hub = end & (hub_index >= 0) & (hub_index < HUBS)

    loads = [
        pltpu.make_async_copy(density, ext.at[pl.ds(0, 2), pl.ds(0, rows), main], load_sem.at[0]),
        pltpu.make_async_copy(velocity, ext.at[pl.ds(2, 3), pl.ds(0, rows), main], load_sem.at[1]),
        pltpu.make_async_copy(bfield, ext.at[pl.ds(5, 3), pl.ds(0, rows), main], load_sem.at[2]),
    ]
    width = half_n * wide
    near = pl.ds(pl.multiple_of(half * width, 16), width)
    far = pl.ds(pl.multiple_of((1 - half) * width, 16), width)
    mine = pl.ds(pl.multiple_of(half * half_n * cols, 128), half_n * cols)
    both = pl.ds(0, 2)
    modes = pl.ds(0, 2 * KMAX)
    table_loads = [
        pltpu.make_async_copy(fwd_hbm.at[both, modes, mine], fwd, load_sem.at[3]),
        pltpu.make_async_copy(back_hbm.at[both, near], back.at[0], load_sem.at[4]),
        pltpu.make_async_copy(back_hbm.at[both, far], back.at[1], load_sem.at[5]),
    ]
    for copy in loads + table_loads:
        copy.start()

    barrier = pltpu.get_barrier_semaphore()

    def other(d):
        return lax.rem(me + d, n)

    def greet(device):
        pl.semaphore_signal(barrier, inc=1, device_id=device, device_id_type=MESH)

    right, left = other(1), other(n - 1)

    @pl.when(end)
    def _():
        for d in range(1, n):
            greet({"phi": other(d)})

    @pl.when(jnp.logical_not(end))
    def _():
        greet({"phi": right})
        greet({"phi": left})

    @pl.when(t > 0)
    def _():
        greet({"theta": t - 1})

    @pl.when(t < nt - 1)
    def _():
        greet({"theta": t + 1})

    @pl.when(end)
    def _():
        pl.semaphore_wait(barrier, n)

    @pl.when(jnp.logical_not(end))
    def _():
        pl.semaphore_wait(barrier, 4)

    for copy in loads:
        copy.wait()

    def remote(src, dst, send, recv, device):
        return pltpu.make_async_remote_copy(
            src_ref=src, dst_ref=dst, send_sem=send, recv_sem=recv,
            device_id=device, device_id_type=MESH,
        )

    def await_bytes(ref, sem):
        pltpu.make_async_copy(ref, ref, sem).wait()

    def repeat(count, body):
        def step(i, carry):
            body(i)
            return carry

        lax.fori_loop(0, count, step, 0)

    def cap_pair(g):
        later = lax.div(g, pole_groups)
        return jnp.where(north, CAP - 2 - 2 * later, 2 * later)

    def channel(j, g):
        return j * pole_groups + lax.rem(g, pole_groups)

    def cap_slots(j, g):
        return pl.ds(channel(j, g) * CAP + 2 * lax.div(g, pole_groups), 2)

    def forward_copy(j, g):
        src = ext.at[channel(j, g), pl.ds(cap0 + cap_pair(g), 2), main]
        dst = cyc.at[g, both, pl.ds(pl.multiple_of(place * cols, 8), cols)]
        device = half * half_n + hub_place(j)
        return (
            pltpu.make_async_copy(src, dst, fr.at[g, place]),
            remote(src, dst, fs.at[j, g], fr.at[g, place], {"phi": device}),
        )

    def middle_copy(g):
        partner = jnp.where(half == 0, half_n, half_n - HUBS) + hub_index
        return remote(part.at[g], other_part.at[g], ms.at[g], mr.at[g], {"phi": partner})

    def target(d):
        spot = lax.rem(place + d, half_n)
        return spot, half * half_n + spot

    def return_copy(g, d):
        spot, device = target(d)
        src = fil.at[g, both, spot]
        dst = caps.at[cap_slots(hub_index, g)]
        sem = rr.at[hub_index, g]
        if d == 0:
            return pltpu.make_async_copy(src, dst, sem)
        return remote(src, dst, rs.at[g, d], sem, {"phi": device})

    ghost_row = jnp.where(north, rows + 2, rows)

    def ghost_copy(g, d):
        spot, device = target(d)
        src = gfil.at[g, jnp.where(north, 0, 1), spot]
        dst = ext.at[channel(hub_index, g), ghost_row]
        sem = gr.at[hub_index, g]
        if d == 0:
            return pltpu.make_async_copy(src, dst, sem)
        return remote(src, dst, gs.at[g, d], sem, {"phi": device})

    second_hub, second_group = BTHETA // pole_groups, BTHETA % pole_groups

    def second_copy(d):
        spot, device = target(d)
        src = gfil.at[second_group, 0, spot]
        dst = ext.at[BTHETA, rows + 1]
        if d == 0:
            return pltpu.make_async_copy(src, dst, g2r.at[0])
        return remote(src, dst, g2s.at[d], g2r.at[0], {"phi": device})

    for c in range(CHANNELS):
        to_right[c] = ext[c, 0:rows, cols - 1]
        to_left[c] = ext[c, 0:rows, 0]
    to_left[CHANNELS] = ext[BPHI, 0:rows, 1]

    go_right = remote(to_right, at_left, hs.at[0], hr.at[0], {"phi": right})
    go_left = remote(to_left, at_right, hs.at[1], hr.at[1], {"phi": left})
    go_right.start()
    go_left.start()

    @pl.when(end)
    def _():
        def send(g):
            for j in range(HUBS):
                here, away = forward_copy(j, g)

                @pl.when(hub_place(j) == place)
                def _():
                    here.start()

                @pl.when(hub_place(j) != place)
                def _():
                    away.start()

        repeat(groups, send)

    go_right.wait()
    go_left.wait()

    def unpack(lo, hi):
        for c in range(CHANNELS):
            ext[c, lo:hi, wide - 1] = at_left[c, lo:hi]
            ext[c, lo:hi, cols] = at_right[c, lo:hi]
        ext[BPHI, lo:hi, cols + 1] = at_right[CHANNELS, lo:hi]

    @pl.when(north)
    def _():
        unpack(CAP, rows)

    @pl.when(south)
    def _():
        unpack(0, rows - CAP)

    @pl.when(jnp.logical_not(end))
    def _():
        unpack(0, rows)

    every = pl.ds(0, CHANNELS)
    down = remote(ext.at[every, rows - 1], ext.at[every, rows + 2], ts.at[0], tr.at[0], {"theta": t + 1})
    up = remote(ext.at[every, 0], ext.at[every, rows], ts.at[1], tr.at[1], {"theta": t - 1})
    up2 = remote(ext.at[BTHETA, 1], ext.at[BTHETA, rows + 1], ts.at[2], tr.at[2], {"theta": t - 1})

    @pl.when(t < nt - 1)
    def _():
        down.start()

    @pl.when(t > 0)
    def _():
        up.start()
        up2.start()

    for copy in table_loads:
        copy.wait()

    @pl.when(hub)
    def _():
        pole = jnp.where(north, 0, 1)
        mode = lax.rem(lax.broadcasted_iota(jnp.int32, (2 * KMAX, 128), 0), KMAX)
        weight = jnp.where(mode == 0, 1.0 / cycle, 2.0 / cycle)

        def analyse(g):
            for i in range(half_n):
                await_bytes(cyc.at[g, both, pl.ds(i * cols, cols)], fr.at[g, i])
            part[g] = product(fwd, jnp.concatenate([cyc[g, 0], cyc[g, 1]], axis=1))
            middle_copy(g).start()

        def evaluate(g):
            await_bytes(other_part.at[g], mr.at[g])
            masks = []
            for s in range(2):
                limit = lax.shift_right_logical(jnp.int32(KMAX), levels[pole, cap_pair(g) + s])
                masks.append(jnp.where(mode < limit, weight, 0.0))
            coeffs = (part[g] + other_part[g]) * jnp.concatenate(masks, axis=1)
            values = product(back[0], coeffs)
            fil[g, 0] = values[:, :128].reshape(half_n, wide, 128)
            fil[g, 1] = values[:, 128:].reshape(half_n, wide, 128)
            for d in reversed(range(half_n)):
                return_copy(g, d).start()

            @pl.when(g >= pole_groups)
            def _():
                k = g - pole_groups
                ghosts = product(back[1], coeffs)
                gfil[k, 0] = ghosts[:, :128].reshape(half_n, wide, 128)
                gfil[k, 1] = ghosts[:, 128:].reshape(half_n, wide, 128)
                for d in reversed(range(half_n)):
                    ghost_copy(k, d).start()

        def step(g):
            @pl.when(g < groups)
            def _():
                analyse(g)

            @pl.when(g >= 1)
            def _():
                evaluate(g - 1)

        repeat(groups + 1, step)

    @pl.when(south & hub & (hub_index == second_hub))
    def _():
        for d in range(half_n):
            second_copy(d).start()

    @pl.when(t > 0)
    def _():
        down.wait_recv()

    @pl.when(t < nt - 1)
    def _():
        up.wait_recv()
        up2.wait_recv()

    def sweep(lo, hi):
        def body(row, carry):
            stencil_row(ext, dout, bout, row, rows, cols)
            return carry

        lax.fori_loop(lo, hi, body, 0)

    early_lo = jnp.where(north, CAP + 1, 0)
    early_hi = jnp.where(south, rows - CAP - 2, rows)
    sweep(early_lo, early_hi)

    @pl.when(end)
    def _():
        def sent(g):
            for j in range(HUBS):
                @pl.when(hub_place(j) != place)
                def _():
                    forward_copy(j, g)[1].wait_send()

        repeat(groups, sent)

        def take(first):
            def one(k):
                g = first + k
                for j in range(HUBS):
                    slots = cap_slots(j, g)
                    await_bytes(caps.at[slots], rr.at[j, g])
                    c = channel(j, g)
                    slot = c * CAP + 2 * lax.div(g, pole_groups)
                    r = cap0 + cap_pair(g)
                    ext[c, r] = caps[slot]
                    ext[c, r + 1] = caps[slot + 1]

            repeat(pole_groups, one)

        take(0)
        sweep(jnp.where(north, CAP - 1, rows - CAP - 2), jnp.where(north, CAP + 1, rows - CAP))
        take(pole_groups)

        def ghost(k):
            for j in range(HUBS):
                await_bytes(ext.at[channel(j, k), ghost_row], gr.at[j, k])

        repeat(pole_groups, ghost)
        for c in ODD:
            ext[c, ghost_row] = -ext[c, ghost_row]

        @pl.when(south)
        def _():
            await_bytes(ext.at[BTHETA, rows + 1], g2r.at[0])
            ext[BTHETA, rows + 1] = -ext[BTHETA, rows + 1]

        sweep(jnp.where(north, 0, rows - CAP), jnp.where(north, CAP - 1, rows))

    @pl.when(t < nt - 1)
    def _():
        down.wait_send()

    @pl.when(t > 0)
    def _():
        up.wait_send()
        up2.wait_send()

    @pl.when(hub)
    def _():
        def drain(g):
            middle_copy(g).wait_send()
            for d in range(1, half_n):
                return_copy(g, d).wait_send()

        def drain_ghost(g):
            for d in range(1, half_n):
                ghost_copy(g, d).wait_send()

        repeat(groups, drain)
        repeat(pole_groups, drain_ghost)

    @pl.when(south & hub & (hub_index == second_hub))
    def _():
        for d in range(1, half_n):
            second_copy(d).wait_send()


def local(n, nt, density, velocity, bfield, levels):
    _, rows, cols, radial = density.shape
    half_n = n // 2
    groups = CHANNELS // HUBS * 2
    wide = cols + 8
    forward, back = tables(n, cols)
    any_space = pl.BlockSpec(memory_space=pl.ANY)
    vmem = pl.BlockSpec(memory_space=pltpu.VMEM)
    f32, bf16 = jnp.float32, jnp.bfloat16
    dma = pltpu.SemaphoreType.DMA
    return pl.pallas_call(
        functools.partial(kernel, n, nt, rows, cols),
        out_shape=(
            jax.ShapeDtypeStruct(density.shape, f32),
            jax.ShapeDtypeStruct(bfield.shape, f32),
        ),
        in_specs=[any_space] * 3 + [pl.BlockSpec(memory_space=pltpu.SMEM)] + [any_space] * 2,
        out_specs=(vmem, vmem),
        scratch_shapes=[
            pltpu.VMEM((CHANNELS, rows + 3, wide, radial), f32),
            pltpu.VMEM((groups, 2, half_n * cols, radial), f32),
            pltpu.VMEM((groups, 2 * KMAX, 2 * radial), f32),
            pltpu.VMEM((groups, 2 * KMAX, 2 * radial), f32),
            pltpu.VMEM((groups, 2, half_n, wide, radial), f32),
            pltpu.VMEM((groups // 2, 2, half_n, wide, radial), f32),
            pltpu.VMEM((CHANNELS * CAP, wide, radial), f32),
            pltpu.VMEM((2, 2 * KMAX, half_n * cols), bf16),
            pltpu.VMEM((2, 2, half_n * wide, 2 * KMAX), bf16),
            pltpu.VMEM((CHANNELS, rows, radial), f32),
            pltpu.VMEM((CHANNELS + 1, rows, radial), f32),
            pltpu.VMEM((CHANNELS, rows, radial), f32),
            pltpu.VMEM((CHANNELS + 1, rows, radial), f32),
            dma((6,)),
            dma((HUBS, groups)),
            dma((groups, half_n)),
            dma((groups,)),
            dma((groups,)),
            dma((groups, half_n)),
            dma((HUBS, groups)),
            dma((groups // 2, half_n)),
            dma((HUBS, groups // 2)),
            dma((half_n,)),
            dma((1,)),
            dma((2,)),
            dma((2,)),
            dma((3,)),
            dma((3,)),
        ],
        compiler_params=pltpu.CompilerParams(
            collective_id=0, has_side_effects=True, vmem_limit_bytes=60 * 1024 * 1024
        ),
        name="substep",
    )(density, velocity, bfield, levels, jnp.asarray(forward), jnp.asarray(back))


def solution(mesh):
    spec = P(None, "theta", "phi", None)
    return jax.shard_map(
        functools.partial(local, mesh.shape["phi"], mesh.shape["theta"]),
        mesh=mesh,
        in_specs=(spec, spec, spec, P()),
        out_specs=(spec, spec),
        check_vma=False,
    )
```

time: 63.5 us -> 55.3 us (0.87)
  local copies, waits for them, and re-layouts: 8.53 us -> 3.18 us
  Pallas kernels: 53.7 us -> 51.4 us
    unnamed x14 -> x4, local copies, waits for them, and re-layouts: 8.53 us -> 3.18 us
    pallas_call x1, Pallas kernels: 53.7 us -> 51.4 us  [local(): pl.pallas_call(functools.partial(kernel, n, nt, rows, cols), out_shape=(j...]
where the time goes in v3:
time: 55.3 us; the launch traced here: 55.2 us
  Pallas kernels  51.4 us (93%)
  local copies, waits for them, and re-layouts  3.18 us (6%)
  between operations  0.65 us (1%)
    pallas_call x1, Pallas kernels, local(): pl.pallas_call(functools.partial(kernel, n, nt, rows, cols), out_shape=(j...  51.4 us
    unnamed x4, local copies, waits for them, and re-layouts  3.18 us

profile of v3, /device:TPU:0, one launch (start us, length us, event | category | flops | bytes accessed | tf_op | source)
XLA Modules:
  0.0 55.2 jit_solution(16089197579742947542)
XLA Ops:
  0.6 51.4 %substep.1 = (f32[2,8,96,128]{3,2,1,0:T(8,128)}, f32[3,8,96,128]{3,2,1,0:T(8,128)}) custom-call(f32[2,8,96,128]{3,2,1,0:T(8,128)} %density.1, f32[3,8,96,128]{3,2,1,0:T(8,128)} %velocity.1, f32[3,8,96,128]{3,2,1,0:T(8,128)} %bfield.1, s32[2,4]{1,0:T(2,128)} %levels.1, bf16[2,256,768]{2,1,0:T(8,128)(2,1)} %constant.4.clone.fwd_hbm, ...), custom_call_target="tpu_custom_call" | custom-call | tf_op jit(solution)/shard_map/substep/pallas_call | solution.py:504
  52.0 0.0 copy-start
  52.0 2.2 %copy.10 = f32[2,8,96,128]{3,2,1,0:T(8,128)} copy(f32[2,8,96,128]{3,2,1,0:T(8,128)} %get-tuple-element.4) | data formatting | bytes 1572864
  54.2 0.0 copy-done
  54.2 1.0 %copy.11 = f32[3,8,96,128]{3,2,1,0:T(8,128)} copy(f32[3,8,96,128]{3,2,1,0:T(8,128)S(1)} %copy-done) | data formatting | bytes 2359296
Async XLA Ops:
  52.0 2.2 %copy-start = (f32[3,8,96,128]{3,2,1,0:T(8,128)S(1)}, f32[3,8,96,128]{3,2,1,0:T(8,128)}, u32[]{:S(2)}) copy-start(f32[3,8,96,128]{3,2,1,0:T(8,128)} %get-tuple-element.5) | copy-start | bytes 3538948

commit v4 on v3

--- a/solution.py
+++ b/solution.py
@@ -14,7 +14,7 @@
 KMAX = 128
 TIME_STEP = 0.2
 CHANNELS = 8
-HUBS = 2
+HUBS = 4
 ODD = (3, 4, 6, 7)
 BTHETA = 6
 BPHI = 7
@@ -540,7 +540,7 @@
             dma((3,)),
         ],
         compiler_params=pltpu.CompilerParams(
-            collective_id=0, has_side_effects=True, vmem_limit_bytes=60 * 1024 * 1024
+            collective_id=0, has_side_effects=True, vmem_limit_bytes=56 * 1024 * 1024
         ),
         name="substep",
     )(density, velocity, bfield, levels, jnp.asarray(forward), jnp.asarray(back))

time: 55.3 us -> 52.9 us (0.957)
  Pallas kernels: 51.4 us -> 48.9 us
    pallas_call x1, Pallas kernels: 51.4 us -> 48.9 us  [local(): pl.pallas_call(functools.partial(kernel, n, nt, rows, cols), out_shape=(j...]
where the time goes in v4:
time: 52.9 us; the launch traced here: 52.7 us
  Pallas kernels  48.9 us (92%)
  local copies, waits for them, and re-layouts  3.18 us (6%)
  between operations  0.65 us (1%)
    pallas_call x1, Pallas kernels, local(): pl.pallas_call(functools.partial(kernel, n, nt, rows, cols), out_shape=(j...  48.9 us
    unnamed x4, local copies, waits for them, and re-layouts  3.18 us

profile of v4, /device:TPU:0, one launch (start us, length us, event | category | flops | bytes accessed | tf_op | source)
XLA Modules:
  0.0 52.7 jit_solution(6502729193981522738)
XLA Ops:
  0.6 48.9 %substep.1 = (f32[2,8,96,128]{3,2,1,0:T(8,128)}, f32[3,8,96,128]{3,2,1,0:T(8,128)}) custom-call(f32[2,8,96,128]{3,2,1,0:T(8,128)} %density.1, f32[3,8,96,128]{3,2,1,0:T(8,128)} %velocity.1, f32[3,8,96,128]{3,2,1,0:T(8,128)} %bfield.1, s32[2,4]{1,0:T(2,128)} %levels.1, bf16[2,256,768]{2,1,0:T(8,128)(2,1)} %constant.4.clone.fwd_hbm, ...), custom_call_target="tpu_custom_call" | custom-call | tf_op jit(solution)/shard_map/substep/pallas_call | solution.py:504
  49.6 0.0 copy-start
  49.6 2.2 %copy.10 = f32[2,8,96,128]{3,2,1,0:T(8,128)} copy(f32[2,8,96,128]{3,2,1,0:T(8,128)} %get-tuple-element.4) | data formatting | bytes 1572864
  51.7 0.0 copy-done
  51.7 1.0 %copy.11 = f32[3,8,96,128]{3,2,1,0:T(8,128)} copy(f32[3,8,96,128]{3,2,1,0:T(8,128)S(1)} %copy-done) | data formatting | bytes 2359296
Async XLA Ops:
  49.6 2.2 %copy-start = (f32[3,8,96,128]{3,2,1,0:T(8,128)S(1)}, f32[3,8,96,128]{3,2,1,0:T(8,128)}, u32[]{:S(2)}) copy-start(f32[3,8,96,128]{3,2,1,0:T(8,128)} %get-tuple-element.5) | copy-start | bytes 3538948

commit v5 on v4

--- a/solution.py
+++ b/solution.py
@@ -39,80 +39,94 @@
     return split_table(forward), split_table(back)
 
 
-def flux(ql, qr, vl, vr):
-    return 0.5 * (ql * vl + qr * vr) - 0.5 * jnp.maximum(jnp.abs(vl), jnp.abs(vr)) * (qr - ql)
-
-
-def stencil_row(ext, dout, bout, row, rows, cols):
-    wide = cols + 8
+def roll_left(x):
+    return pltpu.roll(x, 1, 0)
+
+
+def roll_right(x):
+    return pltpu.roll(x, x.shape[0] - 1, 0)
+
+
+def roll_below(x):
+    return pltpu.roll(x, 1, 1)
+
+
+def roll_above(x):
+    return pltpu.roll(x, x.shape[1] - 1, 1)
+
+
+def lanes(cols):
+    lane = lax.broadcasted_iota(jnp.int32, (cols + 8, 128), 1)
+    return lane == 0, lane == 127
+
+
+def emf_row(ext, emf, j, rows, cols):
+    first, last = lanes(cols)
+    at = jnp.where(j < 0, rows + 2, j)
+    ur, ut, up = ext[2, at], ext[3, at], ext[4, at]
+    br, bt, bp = ext[5, at], ext[6, at], ext[7, at]
+    bt_s = bt + ext[6, j + 1]
+    br_s = br + jnp.where(last, br, roll_above(br))
+    e_p = ut * br_s - ur * bt_s
+    emf[0, j + 1] = e_p
+    e_p0 = ut * (br + br) - ur * bt_s
+    emf[1, j + 1] = e_p + jnp.where(first, e_p0, roll_below(e_p))
+    e_r = up * bt_s - ut * (bp + roll_right(bp))
+    emf[2, j + 1] = e_r + roll_left(e_r)
+
+
+def flux_weights(hl, hr):
+    most = jnp.maximum(jnp.abs(hl), jnp.abs(hr))
+    return hl + most, hr - most
+
+
+def stencil_row(ext, emf, dout, bout, row, rows, cols):
+    first, last = lanes(cols)
     lower = jnp.where(row == 0, rows + 2, row - 1)
     upper = row + 1
-    upper2 = row + 2
-    lane = lax.broadcasted_iota(jnp.int32, (wide, 128), 1)
-    first = lane == 0
-    last = lane == 127
-
-    def from_left(x):
-        return pltpu.roll(x, 1, 0)
-
-    def from_right(x):
-        return pltpu.roll(x, wide - 1, 0)
-
-    def from_below(x):
-        return pltpu.roll(x, 1, 1)
-
-    def from_above(x):
-        return pltpu.roll(x, 127, 1)
-
-    vr, vt, vp = ext[2, row], ext[3, row], ext[4, row]
-    vt_lo, vt_up = ext[3, lower], ext[3, upper]
-    vp_l = from_left(vp)
-    vr_b = jnp.where(first, vr, from_below(vr))
+
+    vr, vp = ext[2, row], ext[4, row]
+    ht = 0.5 * ext[3, row]
+    lo_l, lo_r = flux_weights(0.5 * ext[3, lower], ht)
+    up_l, up_r = flux_weights(ht, 0.5 * ext[3, upper])
+    middle = up_l - lo_r
+    hp = 0.5 * vp
+    p_l, p_r = flux_weights(roll_left(hp), hp)
+    hr = 0.5 * vr
+    r_l, r_r = flux_weights(jnp.where(first, hr, roll_below(hr)), hr)
     for c in range(2):
         q = ext[c, row]
-        tend = flux(q, ext[c, upper], vt, vt_up) - flux(ext[c, lower], q, vt_lo, vt)
-        fp = flux(from_left(q), q, vp_l, vp)
-        tend = tend + from_right(fp) - fp
-        fr = flux(jnp.where(first, q, from_below(q)), q, vr_b, vr)
-        tend = tend + jnp.where(last, q * vr, from_above(fr)) - fr
-        new = q - TIME_STEP * tend
-        dout[c, row] = new[:cols]
-
-    def emfs(j, bt_next):
-        ur, ut, up = ext[2, j], ext[3, j], ext[4, j]
-        br, bt, bp = ext[5, j], ext[6, j], ext[7, j]
-        br_c = 0.5 * (br + jnp.where(last, br, from_above(br)))
-        bt_c = 0.5 * (bt + bt_next)
-        bp_c = 0.5 * (bp + from_right(bp))
-        e_r = -(ut * bp_c - up * bt_c)
-        e_p = -(ur * bt_c - ut * br_c)
-        e_p0 = -(ur * bt_c - ut * br)
-        pair_p = e_p + jnp.where(first, e_p0, from_below(e_p))
-        pair_r = e_r + from_left(e_r)
-        return e_p, pair_p, pair_r, br_c, bp_c
-
-    bt = ext[6, row]
-    bt_up = ext[6, upper]
-    ep_lo, pp_lo, pr_lo, _, _ = emfs(lower, bt)
-    ep, pp, pr, br_c, bp_c = emfs(row, bt_up)
-    ep_up, pp_up, pr_up, _, _ = emfs(upper, ext[6, upper2])
-    br = ext[5, row]
-    e_t = -(vp * br_c - vr * bp_c)
-    e_t0 = -(vp * br - vr * bp_c)
-    et_pair = e_t + from_left(e_t)
-    et_pair0 = e_t0 + from_left(e_t0)
-    edge_t = et_pair + jnp.where(first, et_pair0, from_below(et_pair))
-    edge_t_above = jnp.where(last, 2.0 * et_pair, from_above(edge_t))
-    edge_p = pp_lo + pp
-    edge_p_above = jnp.where(last, 2.0 * (ep_lo + ep), from_above(edge_p))
-    edge_r = pr_lo + pr
-    scale = TIME_STEP * 0.25
-    new_r = br - scale * ((pp_up - pp_lo) - (from_right(edge_t) - edge_t))
-    new_t = bt - scale * ((from_right(edge_r) - edge_r) - (edge_p_above - edge_p))
-    new_p = ext[7, row] - scale * ((edge_t_above - edge_t) - (pr_up - pr_lo))
+        tend = middle * q + (up_r * ext[c, upper] - lo_l * ext[c, lower])
+        fp = p_l * roll_left(q) + p_r * q
+        fr = r_l * jnp.where(first, q, roll_below(q)) + r_r * q
+        tend = tend + (roll_right(fp) - fp)
+        tend = tend + (jnp.where(last, q * vr, roll_above(fr)) - fr)
+        dout[c, row] = (q - TIME_STEP * tend)[:cols]
+
+    br, bp = ext[5, row], ext[7, row]
+    bp_s = bp + roll_right(bp)
+    br_s = br + jnp.where(last, br, roll_above(br))
+    vr_bp = vr * bp_s
+    e_t = vr_bp - vp * br_s
+    e_t0 = vr_bp - vp * (br + br)
+    pair = e_t + roll_left(e_t)
+    pair0 = e_t0 + roll_left(e_t0)
+    edge_t = pair + jnp.where(first, pair0, roll_below(pair))
+    scale = TIME_STEP * 0.125
+    new_r = br - scale * (
+        (emf[1, row + 2] - emf[1, row]) - (roll_right(edge_t) - edge_t)
+    )
     bout[0, row] = new_r[:cols]
+    edge_t_above = jnp.where(last, 2.0 * pair, roll_above(edge_t))
+    new_p = bp - scale * ((edge_t_above - edge_t) - (emf[2, row + 2] - emf[2, row]))
+    bout[2, row] = new_p[:cols]
+    edge_p = emf[1, row] + emf[1, row + 1]
+    edge_p_above = jnp.where(last, 2.0 * (emf[0, row] + emf[0, row + 1]), roll_above(edge_p))
+    edge_r = emf[2, row] + emf[2, row + 1]
+    new_t = ext[6, row] - scale * (
+        (roll_right(edge_r) - edge_r) - (edge_p_above - edge_p)
+    )
     bout[1, row] = new_t[:cols]
-    bout[2, row] = new_p[:cols]
 
 
 def split(x):
@@ -130,7 +144,7 @@
     n, nt, rows, cols,
     density, velocity, bfield, levels, fwd_hbm, back_hbm,
     dout, bout,
-    ext, cyc, part, other_part, fil, gfil, caps, fwd, back, to_right, to_left, at_left, at_right,
+    ext, emf, cyc, part, other_part, fil, gfil, caps, fwd, back, to_right, to_left, at_left, at_right,
     load_sem, fs, fr, ms, mr, rs, rr, gs, gr, g2s, g2r, hs, hr, ts, tr,
 ):
     half_n = n // 2
@@ -349,6 +363,35 @@
     for copy in table_loads:
         copy.wait()
 
+    def sweep(lo, hi):
+        def body(row, carry):
+            stencil_row(ext, emf, dout, bout, row, rows, cols)
+            return carry
+
+        lax.fori_loop(lo, hi, body, 0)
+
+    def make_emfs(lo, hi):
+        def body(j, carry):
+            emf_row(ext, emf, j, rows, cols)
+            return carry
+
+        lax.fori_loop(lo, hi, body, 0)
+
+    early_lo = jnp.where(north, CAP + 1, 0)
+    early_hi = jnp.where(south, rows - CAP - 2, rows)
+
+    def ready():
+        @pl.when(t > 0)
+        def _():
+            down.wait_recv()
+
+        @pl.when(t < nt - 1)
+        def _():
+            up.wait_recv()
+            up2.wait_recv()
+
+        make_emfs(jnp.where(north, CAP, -1), jnp.where(south, rows - CAP - 1, rows + 1))
+
     @pl.when(hub)
     def _():
         pole = jnp.where(north, 0, 1)
@@ -388,36 +431,28 @@
             def _():
                 analyse(g)
 
+            @pl.when(g == 1)
+            def _():
+                ready()
+
             @pl.when(g >= 1)
             def _():
+                row = early_lo + g - 1
+                sweep(row, jnp.minimum(row + 1, early_hi))
                 evaluate(g - 1)
 
         repeat(groups + 1, step)
+        sweep(early_lo + groups, early_hi)
 
     @pl.when(south & hub & (hub_index == second_hub))
     def _():
         for d in range(half_n):
             second_copy(d).start()
 
-    @pl.when(t > 0)
-    def _():
-        down.wait_recv()
-
-    @pl.when(t < nt - 1)
-    def _():
-        up.wait_recv()
-        up2.wait_recv()
-
-    def sweep(lo, hi):
-        def body(row, carry):
-            stencil_row(ext, dout, bout, row, rows, cols)
-            return carry
-
-        lax.fori_loop(lo, hi, body, 0)
-
-    early_lo = jnp.where(north, CAP + 1, 0)
-    early_hi = jnp.where(south, rows - CAP - 2, rows)
-    sweep(early_lo, early_hi)
+    @pl.when(jnp.logical_not(hub))
+    def _():
+        ready()
+        sweep(early_lo, early_hi)
 
     @pl.when(end)
     def _():
@@ -444,6 +479,9 @@
             repeat(pole_groups, one)
 
         take(0)
+        make_emfs(
+            jnp.where(north, CAP - 2, rows - CAP - 1), jnp.where(north, CAP, rows - CAP + 1)
+        )
         sweep(jnp.where(north, CAP - 1, rows - CAP - 2), jnp.where(north, CAP + 1, rows - CAP))
         take(pole_groups)
 
@@ -460,6 +498,7 @@
             await_bytes(ext.at[BTHETA, rows + 1], g2r.at[0])
             ext[BTHETA, rows + 1] = -ext[BTHETA, rows + 1]
 
+        make_emfs(jnp.where(north, -1, rows - CAP + 1), jnp.where(north, CAP - 2, rows + 1))
         sweep(jnp.where(north, 0, rows - CAP), jnp.where(north, CAP - 1, rows))
 
     @pl.when(t < nt - 1)
@@ -511,6 +550,7 @@
         out_specs=(vmem, vmem),
         scratch_shapes=[
             pltpu.VMEM((CHANNELS, rows + 3, wide, radial), f32),
+            pltpu.VMEM((3, rows + 2, wide, radial), f32),
             pltpu.VMEM((groups, 2, half_n * cols, radial), f32),
             pltpu.VMEM((groups, 2 * KMAX, 2 * radial), f32),
             pltpu.VMEM((groups, 2 * KMAX, 2 * radial), f32),

time: 52.9 us -> 52.9 us (level)
  no operation moved by 1% of the time
where the time goes in v5:
time: 52.9 us; the launch traced here: 52.7 us
  Pallas kernels  48.9 us (92%)
  local copies, waits for them, and re-layouts  3.18 us (6%)
  between operations  0.65 us (1%)
    pallas_call x1, Pallas kernels, local(): pl.pallas_call(functools.partial(kernel, n, nt, rows, cols), out_shape=(j...  48.9 us
    unnamed x4, local copies, waits for them, and re-layouts  3.18 us

profile of v5, /device:TPU:0, one launch (start us, length us, event | category | flops | bytes accessed | tf_op | source)
XLA Modules:
  0.0 52.7 jit_solution(8964707607435969430)
XLA Ops:
  0.6 48.9 %substep.1 = (f32[2,8,96,128]{3,2,1,0:T(8,128)}, f32[3,8,96,128]{3,2,1,0:T(8,128)}) custom-call(f32[2,8,96,128]{3,2,1,0:T(8,128)} %density.1, f32[3,8,96,128]{3,2,1,0:T(8,128)} %velocity.1, f32[3,8,96,128]{3,2,1,0:T(8,128)} %bfield.1, s32[2,4]{1,0:T(2,128)} %levels.1, bf16[2,256,768]{2,1,0:T(8,128)(2,1)} %constant.4.clone.fwd_hbm, ...), custom_call_target="tpu_custom_call" | custom-call | tf_op jit(solution)/shard_map/substep/pallas_call | solution.py:543
  49.5 0.0 copy-start
  49.5 2.2 %copy.10 = f32[2,8,96,128]{3,2,1,0:T(8,128)} copy(f32[2,8,96,128]{3,2,1,0:T(8,128)} %get-tuple-element.4) | data formatting | bytes 1572864
  51.7 0.0 copy-done
  51.7 1.0 %copy.11 = f32[3,8,96,128]{3,2,1,0:T(8,128)} copy(f32[3,8,96,128]{3,2,1,0:T(8,128)S(1)} %copy-done) | data formatting | bytes 2359296
Async XLA Ops:
  49.5 2.2 %copy-start = (f32[3,8,96,128]{3,2,1,0:T(8,128)S(1)}, f32[3,8,96,128]{3,2,1,0:T(8,128)}, u32[]{:S(2)}) copy-start(f32[3,8,96,128]{3,2,1,0:T(8,128)} %get-tuple-element.5) | copy-start | bytes 3538948

commit v6 on v5

--- a/solution.py
+++ b/solution.py
@@ -15,6 +15,8 @@
 TIME_STEP = 0.2
 CHANNELS = 8
 HUBS = 4
+SHARE = (1, 1, 3, 3)
+BASE = (0, 1, 2, 5)
 ODD = (3, 4, 6, 7)
 BTHETA = 6
 BPHI = 7
@@ -148,8 +150,6 @@
     load_sem, fs, fr, ms, mr, rs, rr, gs, gr, g2s, g2r, hs, hr, ts, tr,
 ):
     half_n = n // 2
-    groups = CHANNELS // HUBS * 2
-    pole_groups = groups // 2
     wide = cols + 8
     cycle = n * cols
     t = lax.axis_index("theta")
@@ -163,10 +163,18 @@
     place = lax.rem(me, half_n)
 
     def hub_place(j):
-        return jnp.where(half == 0, half_n - HUBS + j, j)
-
-    hub_index = place - hub_place(0)
-    hub = end & (hub_index >= 0) & (hub_index < HUBS)
+        return jnp.where(half == 0, half_n - HUBS + j, (j + 2) % HUBS)
+
+    hub = end & jnp.where(half == 0, place >= half_n - HUBS, place < HUBS)
+    hub_index = jnp.where(half == 0, place - (half_n - HUBS), lax.rem(place + 2, HUBS))
+
+    def share(j):
+        return SHARE[j] if isinstance(j, int) else jnp.where(j < 2, 1, 3)
+
+    def base(j):
+        return BASE[j] if isinstance(j, int) else jnp.where(j < 2, j, 3 * j - 4)
+
+    my_share = share(hub_index)
 
     loads = [
         pltpu.make_async_copy(density, ext.at[pl.ds(0, 2), pl.ds(0, rows), main], load_sem.at[0]),
@@ -242,18 +250,18 @@
 
         lax.fori_loop(0, count, step, 0)
 
-    def cap_pair(g):
-        later = lax.div(g, pole_groups)
+    def cap_pair(j, g):
+        later = lax.div(g, share(j))
         return jnp.where(north, CAP - 2 - 2 * later, 2 * later)
 
     def channel(j, g):
-        return j * pole_groups + lax.rem(g, pole_groups)
+        return base(j) + lax.rem(g, share(j))
 
     def cap_slots(j, g):
-        return pl.ds(channel(j, g) * CAP + 2 * lax.div(g, pole_groups), 2)
+        return pl.ds(channel(j, g) * CAP + 2 * lax.div(g, share(j)), 2)
 
     def forward_copy(j, g):
-        src = ext.at[channel(j, g), pl.ds(cap0 + cap_pair(g), 2), main]
+        src = ext.at[channel(j, g), pl.ds(cap0 + cap_pair(j, g), 2), main]
         dst = cyc.at[g, both, pl.ds(pl.multiple_of(place * cols, 8), cols)]
         device = half * half_n + hub_place(j)
         return (
@@ -262,7 +270,7 @@
         )
 
     def middle_copy(g):
-        partner = jnp.where(half == 0, half_n, half_n - HUBS) + hub_index
+        partner = jnp.where(half == 0, half_n + lax.rem(hub_index + 2, HUBS), half_n - HUBS + hub_index)
         return remote(part.at[g], other_part.at[g], ms.at[g], mr.at[g], {"phi": partner})
 
     def target(d):
@@ -289,7 +297,7 @@
             return pltpu.make_async_copy(src, dst, sem)
         return remote(src, dst, gs.at[g, d], sem, {"phi": device})
 
-    second_hub, second_group = BTHETA // pole_groups, BTHETA % pole_groups
+    second_hub, second_group = HUBS - 1, BTHETA - BASE[HUBS - 1]
 
     def second_copy(d):
         spot, device = target(d)
@@ -312,18 +320,19 @@
     @pl.when(end)
     def _():
         def send(g):
-            for j in range(HUBS):
+            for j in reversed(range(HUBS)):
                 here, away = forward_copy(j, g)
-
-                @pl.when(hub_place(j) == place)
+                due = g < 2 * SHARE[j]
+
+                @pl.when(due & (hub_place(j) == place))
                 def _():
                     here.start()
 
-                @pl.when(hub_place(j) != place)
+                @pl.when(due & (hub_place(j) != place))
                 def _():
                     away.start()
 
-        repeat(groups, send)
+        repeat(2 * max(SHARE), send)
 
     go_right.wait()
     go_left.wait()
@@ -408,7 +417,7 @@
             await_bytes(other_part.at[g], mr.at[g])
             masks = []
             for s in range(2):
-                limit = lax.shift_right_logical(jnp.int32(KMAX), levels[pole, cap_pair(g) + s])
+                limit = lax.shift_right_logical(jnp.int32(KMAX), levels[pole, cap_pair(hub_index, g) + s])
                 masks.append(jnp.where(mode < limit, weight, 0.0))
             coeffs = (part[g] + other_part[g]) * jnp.concatenate(masks, axis=1)
             values = product(back[0], coeffs)
@@ -417,9 +426,9 @@
             for d in reversed(range(half_n)):
                 return_copy(g, d).start()
 
-            @pl.when(g >= pole_groups)
+            @pl.when(g >= my_share)
             def _():
-                k = g - pole_groups
+                k = g - my_share
                 ghosts = product(back[1], coeffs)
                 gfil[k, 0] = ghosts[:, :128].reshape(half_n, wide, 128)
                 gfil[k, 1] = ghosts[:, 128:].reshape(half_n, wide, 128)
@@ -427,7 +436,7 @@
                     ghost_copy(k, d).start()
 
         def step(g):
-            @pl.when(g < groups)
+            @pl.when(g < 2 * my_share)
             def _():
                 analyse(g)
 
@@ -441,8 +450,8 @@
                 sweep(row, jnp.minimum(row + 1, early_hi))
                 evaluate(g - 1)
 
-        repeat(groups + 1, step)
-        sweep(early_lo + groups, early_hi)
+        repeat(2 * my_share + 1, step)
+        sweep(early_lo + 2 * my_share, early_hi)
 
     @pl.when(south & hub & (hub_index == second_hub))
     def _():
@@ -458,38 +467,37 @@
     def _():
         def sent(g):
             for j in range(HUBS):
-                @pl.when(hub_place(j) != place)
+                @pl.when((g < 2 * SHARE[j]) & (hub_place(j) != place))
                 def _():
                     forward_copy(j, g)[1].wait_send()
 
-        repeat(groups, sent)
-
-        def take(first):
-            def one(k):
-                g = first + k
-                for j in range(HUBS):
-                    slots = cap_slots(j, g)
-                    await_bytes(caps.at[slots], rr.at[j, g])
+        repeat(2 * max(SHARE), sent)
+
+        def take(later):
+            for j in range(HUBS):
+
+                def one(k):
+                    g = later * SHARE[j] + k
+                    await_bytes(caps.at[cap_slots(j, g)], rr.at[j, g])
                     c = channel(j, g)
-                    slot = c * CAP + 2 * lax.div(g, pole_groups)
-                    r = cap0 + cap_pair(g)
+                    slot = c * CAP + 2 * later
+                    r = cap0 + cap_pair(j, g)
                     ext[c, r] = caps[slot]
                     ext[c, r + 1] = caps[slot + 1]
 
-            repeat(pole_groups, one)
+                repeat(SHARE[j], one)
 
         take(0)
         make_emfs(
             jnp.where(north, CAP - 2, rows - CAP - 1), jnp.where(north, CAP, rows - CAP + 1)
         )
         sweep(jnp.where(north, CAP - 1, rows - CAP - 2), jnp.where(north, CAP + 1, rows - CAP))
-        take(pole_groups)
-
-        def ghost(k):
-            for j in range(HUBS):
+        take(1)
+
+        for j in range(HUBS):
+            for k in range(SHARE[j]):
                 await_bytes(ext.at[channel(j, k), ghost_row], gr.at[j, k])
 
-        repeat(pole_groups, ghost)
         for c in ODD:
             ext[c, ghost_row] = -ext[c, ghost_row]
 
@@ -521,8 +529,8 @@
             for d in range(1, half_n):
                 ghost_copy(g, d).wait_send()
 
-        repeat(groups, drain)
-        repeat(pole_groups, drain_ghost)
+        repeat(2 * my_share, drain)
+        repeat(my_share, drain_ghost)
 
     @pl.when(south & hub & (hub_index == second_hub))
     def _():
@@ -533,7 +541,7 @@
 def local(n, nt, density, velocity, bfield, levels):
     _, rows, cols, radial = density.shape
     half_n = n // 2
-    groups = CHANNELS // HUBS * 2
+    groups = 2 * max(SHARE)
     wide = cols + 8
     forward, back = tables(n, cols)
     any_space = pl.BlockSpec(memory_space=pl.ANY)

time: 52.9 us -> 53.7 us (1.015)
  Pallas kernels: 48.9 us -> 49.8 us
    pallas_call x1, Pallas kernels: 48.9 us -> 49.8 us  [local(): pl.pallas_call(functools.partial(kernel, n, nt, rows, cols), out_shape=(j...]
where the time goes in v6:
time: 53.7 us; the launch traced here: 53.6 us
  Pallas kernels  49.8 us (93%)
  local copies, waits for them, and re-layouts  3.18 us (6%)
  between operations  0.65 us (1%)
    pallas_call x1, Pallas kernels, local(): pl.pallas_call(functools.partial(kernel, n, nt, rows, cols), out_shape=(j...  49.8 us
    unnamed x4, local copies, waits for them, and re-layouts  3.18 us

profile of v6, /device:TPU:0, one launch (start us, length us, event | category | flops | bytes accessed | tf_op | source)
XLA Modules:
  0.0 53.6 jit_solution(6602411122869504364)
XLA Ops:
  0.6 49.8 %substep.1 = (f32[2,8,96,128]{3,2,1,0:T(8,128)}, f32[3,8,96,128]{3,2,1,0:T(8,128)}) custom-call(f32[2,8,96,128]{3,2,1,0:T(8,128)} %density.1, f32[3,8,96,128]{3,2,1,0:T(8,128)} %velocity.1, f32[3,8,96,128]{3,2,1,0:T(8,128)} %bfield.1, s32[2,4]{1,0:T(2,128)} %levels.1, bf16[2,256,768]{2,1,0:T(8,128)(2,1)} %constant.4.clone.fwd_hbm, ...), custom_call_target="tpu_custom_call" | custom-call | tf_op jit(solution)/shard_map/substep/pallas_call | solution.py:551
  50.4 0.0 copy-start
  50.4 2.2 %copy.10 = f32[2,8,96,128]{3,2,1,0:T(8,128)} copy(f32[2,8,96,128]{3,2,1,0:T(8,128)} %get-tuple-element.4) | data formatting | bytes 1572864
  52.6 0.0 copy-done
  52.6 1.0 %copy.11 = f32[3,8,96,128]{3,2,1,0:T(8,128)} copy(f32[3,8,96,128]{3,2,1,0:T(8,128)S(1)} %copy-done) | data formatting | bytes 2359296
Async XLA Ops:
  50.4 2.2 %copy-start = (f32[3,8,96,128]{3,2,1,0:T(8,128)S(1)}, f32[3,8,96,128]{3,2,1,0:T(8,128)}, u32[]{:S(2)}) copy-start(f32[3,8,96,128]{3,2,1,0:T(8,128)} %get-tuple-element.5) | copy-start | bytes 3538948

commit v7 on v5

--- a/solution.py
+++ b/solution.py
@@ -143,8 +143,8 @@
 def kernel(
     n, nt, rows, cols,
     density, velocity, bfield, levels, fwd_hbm, back_hbm,
-    dout, bout,
-    ext, emf, cyc, part, other_part, fil, gfil, caps, fwd, back, to_right, to_left, at_left, at_right,
+    dens_hbm, field_hbm,
+    ext, dout, bout, out_sem, emf, cyc, part, other_part, fil, gfil, caps, fwd, back, to_right, to_left, at_left, at_right,
     load_sem, fs, fr, ms, mr, rs, rr, gs, gr, g2s, g2r, hs, hr, ts, tr,
 ):
     half_n = n // 2
@@ -363,9 +363,17 @@
     for copy in table_loads:
         copy.wait()
 
+    def row_copies(row):
+        return (
+            pltpu.make_async_copy(dout.at[pl.ds(0, 2), row], dens_hbm.at[pl.ds(0, 2), row], out_sem.at[0, row]),
+            pltpu.make_async_copy(bout.at[pl.ds(0, 3), row], field_hbm.at[pl.ds(0, 3), row], out_sem.at[1, row]),
+        )
+
     def sweep(lo, hi):
         def body(row, carry):
             stencil_row(ext, emf, dout, bout, row, rows, cols)
+            for copy in row_copies(row):
+                copy.start()
             return carry
 
         lax.fori_loop(lo, hi, body, 0)
@@ -426,22 +434,15 @@
                 for d in reversed(range(half_n)):
                     ghost_copy(k, d).start()
 
+        repeat(groups, analyse)
+        ready()
+
         def step(g):
-            @pl.when(g < groups)
-            def _():
-                analyse(g)
-
-            @pl.when(g == 1)
-            def _():
-                ready()
-
-            @pl.when(g >= 1)
-            def _():
-                row = early_lo + g - 1
-                sweep(row, jnp.minimum(row + 1, early_hi))
-                evaluate(g - 1)
-
-        repeat(groups + 1, step)
+            row = early_lo + g
+            sweep(row, jnp.minimum(row + 1, early_hi))
+            evaluate(g)
+
+        repeat(groups, step)
         sweep(early_lo + groups, early_hi)
 
     @pl.when(south & hub & (hub_index == second_hub))
@@ -501,6 +502,12 @@
         make_emfs(jnp.where(north, -1, rows - CAP + 1), jnp.where(north, CAP - 2, rows + 1))
         sweep(jnp.where(north, 0, rows - CAP), jnp.where(north, CAP - 1, rows))
 
+    def wait_row(row):
+        for copy in row_copies(row):
+            copy.wait()
+
+    repeat(rows, wait_row)
+
     @pl.when(t < nt - 1)
     def _():
         down.wait_send()
@@ -537,7 +544,6 @@
     wide = cols + 8
     forward, back = tables(n, cols)
     any_space = pl.BlockSpec(memory_space=pl.ANY)
-    vmem = pl.BlockSpec(memory_space=pltpu.VMEM)
     f32, bf16 = jnp.float32, jnp.bfloat16
     dma = pltpu.SemaphoreType.DMA
     return pl.pallas_call(
@@ -547,9 +553,12 @@
             jax.ShapeDtypeStruct(bfield.shape, f32),
         ),
         in_specs=[any_space] * 3 + [pl.BlockSpec(memory_space=pltpu.SMEM)] + [any_space] * 2,
-        out_specs=(vmem, vmem),
+        out_specs=(any_space, any_space),
         scratch_shapes=[
             pltpu.VMEM((CHANNELS, rows + 3, wide, radial), f32),
+            pltpu.VMEM(density.shape, f32),
+            pltpu.VMEM(bfield.shape, f32),
+            dma((2, rows)),
             pltpu.VMEM((3, rows + 2, wide, radial), f32),
             pltpu.VMEM((groups, 2, half_n * cols, radial), f32),
             pltpu.VMEM((groups, 2 * KMAX, 2 * radial), f32),

time: 52.9 us -> 51.4 us (0.972)
  Pallas kernels: 48.9 us -> 47.5 us
    pallas_call x1, Pallas kernels: 48.9 us -> 47.5 us  [local(): pl.pallas_call(functools.partial(kernel, n, nt, rows, cols), out_shape=(j...]
where the time goes in v7:
time: 51.4 us; the launch traced here: 51.3 us
  Pallas kernels  47.5 us (92%)
  local copies, waits for them, and re-layouts  3.18 us (6%)
  between operations  0.65 us (1%)
    pallas_call x1, Pallas kernels, local(): pl.pallas_call(functools.partial(kernel, n, nt, rows, cols), out_shape=(j...  47.5 us
    unnamed x4, local copies, waits for them, and re-layouts  3.18 us

profile of v7, /device:TPU:0, one launch (start us, length us, event | category | flops | bytes accessed | tf_op | source)
XLA Modules:
  0.0 51.3 jit_solution(7440810201423348052)
XLA Ops:
  0.6 47.5 %substep.1 = (f32[2,8,96,128]{3,2,1,0:T(8,128)}, f32[3,8,96,128]{3,2,1,0:T(8,128)}) custom-call(f32[2,8,96,128]{3,2,1,0:T(8,128)} %density.1, f32[3,8,96,128]{3,2,1,0:T(8,128)} %velocity.1, f32[3,8,96,128]{3,2,1,0:T(8,128)} %bfield.1, s32[2,4]{1,0:T(2,128)} %levels.1, bf16[2,256,768]{2,1,0:T(8,128)(2,1)} %constant.4.clone.fwd_hbm, ...), custom_call_target="tpu_custom_call" | custom-call | tf_op jit(solution)/shard_map/substep/pallas_call | solution.py:549
  48.1 0.0 copy-start
  48.1 2.2 %copy.10 = f32[2,8,96,128]{3,2,1,0:T(8,128)} copy(f32[2,8,96,128]{3,2,1,0:T(8,128)} %get-tuple-element.4) | data formatting | bytes 1572864
  50.3 0.0 copy-done
  50.3 1.0 %copy.11 = f32[3,8,96,128]{3,2,1,0:T(8,128)} copy(f32[3,8,96,128]{3,2,1,0:T(8,128)S(1)} %copy-done) | data formatting | bytes 2359296
Async XLA Ops:
  48.1 2.2 %copy-start = (f32[3,8,96,128]{3,2,1,0:T(8,128)S(1)}, f32[3,8,96,128]{3,2,1,0:T(8,128)}, u32[]{:S(2)}) copy-start(f32[3,8,96,128]{3,2,1,0:T(8,128)} %get-tuple-element.5) | copy-start | bytes 3538948

commit v8 on v7

--- a/solution.py
+++ b/solution.py
@@ -184,36 +184,36 @@
         pltpu.make_async_copy(back_hbm.at[both, near], back.at[0], load_sem.at[4]),
         pltpu.make_async_copy(back_hbm.at[both, far], back.at[1], load_sem.at[5]),
     ]
+    barrier = pltpu.get_barrier_semaphore()
+
+    def other(d):
+        return lax.rem(me + d, n)
+
+    def greet(device):
+        pl.semaphore_signal(barrier, inc=1, device_id=device, device_id_type=MESH)
+
+    right, left = other(1), other(n - 1)
+
+    @pl.when(end)
+    def _():
+        for d in range(1, n):
+            greet({"phi": other(d)})
+
+    @pl.when(jnp.logical_not(end))
+    def _():
+        greet({"phi": right})
+        greet({"phi": left})
+
+    @pl.when(t > 0)
+    def _():
+        greet({"theta": t - 1})
+
+    @pl.when(t < nt - 1)
+    def _():
+        greet({"theta": t + 1})
+
     for copy in loads + table_loads:
         copy.start()
-
-    barrier = pltpu.get_barrier_semaphore()
-
-    def other(d):
-        return lax.rem(me + d, n)
-
-    def greet(device):
-        pl.semaphore_signal(barrier, inc=1, device_id=device, device_id_type=MESH)
-
-    right, left = other(1), other(n - 1)
-
-    @pl.when(end)
-    def _():
-        for d in range(1, n):
-            greet({"phi": other(d)})
-
-    @pl.when(jnp.logical_not(end))
-    def _():
-        greet({"phi": right})
-        greet({"phi": left})
-
-    @pl.when(t > 0)
-    def _():
-        greet({"theta": t - 1})
-
-    @pl.when(t < nt - 1)
-    def _():
-        greet({"theta": t + 1})
 
     @pl.when(end)
     def _():
@@ -325,6 +325,19 @@
 
         repeat(groups, send)
 
+    for copy in table_loads:
+        copy.wait()
+
+    @pl.when(hub)
+    def _():
+        def analyse(g):
+            for i in range(half_n):
+                await_bytes(cyc.at[g, both, pl.ds(i * cols, cols)], fr.at[g, i])
+            part[g] = product(fwd, jnp.concatenate([cyc[g, 0], cyc[g, 1]], axis=1))
+            middle_copy(g).start()
+
+        repeat(groups, analyse)
+
     go_right.wait()
     go_left.wait()
 
@@ -359,9 +372,6 @@
     def _():
         up.start()
         up2.start()
-
-    for copy in table_loads:
-        copy.wait()
 
     def row_copies(row):
         return (
@@ -405,12 +415,6 @@
         pole = jnp.where(north, 0, 1)
         mode = lax.rem(lax.broadcasted_iota(jnp.int32, (2 * KMAX, 128), 0), KMAX)
         weight = jnp.where(mode == 0, 1.0 / cycle, 2.0 / cycle)
-
-        def analyse(g):
-            for i in range(half_n):
-                await_bytes(cyc.at[g, both, pl.ds(i * cols, cols)], fr.at[g, i])
-            part[g] = product(fwd, jnp.concatenate([cyc[g, 0], cyc[g, 1]], axis=1))
-            middle_copy(g).start()
 
         def evaluate(g):
             await_bytes(other_part.at[g], mr.at[g])
@@ -434,7 +438,6 @@
                 for d in reversed(range(half_n)):
                     ghost_copy(k, d).start()
 
-        repeat(groups, analyse)
         ready()
 
         def step(g):

time: 51.4 us -> 51.5 us (level)
  no operation moved by 1% of the time
where the time goes in v8:
time: 51.5 us; the launch traced here: 51.4 us
  Pallas kernels  47.6 us (92%)
  local copies, waits for them, and re-layouts  3.18 us (6%)
  between operations  0.65 us (1%)
    pallas_call x1, Pallas kernels, local(): pl.pallas_call(functools.partial(kernel, n, nt, rows, cols), out_shape=(j...  47.6 us
    unnamed x4, local copies, waits for them, and re-layouts  3.18 us

profile of v8, /device:TPU:0, one launch (start us, length us, event | category | flops | bytes accessed | tf_op | source)
XLA Modules:
  0.0 51.4 jit_solution(16227213648595691184)
XLA Ops:
  0.6 47.6 %substep.1 = (f32[2,8,96,128]{3,2,1,0:T(8,128)}, f32[3,8,96,128]{3,2,1,0:T(8,128)}) custom-call(f32[2,8,96,128]{3,2,1,0:T(8,128)} %density.1, f32[3,8,96,128]{3,2,1,0:T(8,128)} %velocity.1, f32[3,8,96,128]{3,2,1,0:T(8,128)} %bfield.1, s32[2,4]{1,0:T(2,128)} %levels.1, bf16[2,256,768]{2,1,0:T(8,128)(2,1)} %constant.4.clone.fwd_hbm, ...), custom_call_target="tpu_custom_call" | custom-call | tf_op jit(solution)/shard_map/substep/pallas_call | solution.py:552
  48.2 0.0 copy-start
  48.2 2.2 %copy.10 = f32[2,8,96,128]{3,2,1,0:T(8,128)} copy(f32[2,8,96,128]{3,2,1,0:T(8,128)} %get-tuple-element.4) | data formatting | bytes 1572864
  50.4 0.0 copy-done
  50.4 1.0 %copy.11 = f32[3,8,96,128]{3,2,1,0:T(8,128)} copy(f32[3,8,96,128]{3,2,1,0:T(8,128)S(1)} %copy-done) | data formatting | bytes 2359296
Async XLA Ops:
  48.2 2.2 %copy-start = (f32[3,8,96,128]{3,2,1,0:T(8,128)S(1)}, f32[3,8,96,128]{3,2,1,0:T(8,128)}, u32[]{:S(2)}) copy-start(f32[3,8,96,128]{3,2,1,0:T(8,128)} %get-tuple-element.5) | copy-start | bytes 3538948

commit v9 on v7

--- a/solution.py
+++ b/solution.py
@@ -101,8 +101,9 @@
         fr = r_l * jnp.where(first, q, roll_below(q)) + r_r * q
         tend = tend + (roll_right(fp) - fp)
         tend = tend + (jnp.where(last, q * vr, roll_above(fr)) - fr)
-        dout[c, row] = (q - TIME_STEP * tend)[:cols]
-
+        dout[c, row] = (q - TIME_STEP * tend)[:cols] - dout[c, row]
+
+    scale = TIME_STEP * 0.125
     br, bp = ext[5, row], ext[7, row]
     bp_s = bp + roll_right(bp)
     br_s = br + jnp.where(last, br, roll_above(br))
@@ -112,21 +113,20 @@
     pair = e_t + roll_left(e_t)
     pair0 = e_t0 + roll_left(e_t0)
     edge_t = pair + jnp.where(first, pair0, roll_below(pair))
-    scale = TIME_STEP * 0.125
     new_r = br - scale * (
         (emf[1, row + 2] - emf[1, row]) - (roll_right(edge_t) - edge_t)
     )
-    bout[0, row] = new_r[:cols]
+    bout[0, row] = new_r[:cols] - bout[0, row]
     edge_t_above = jnp.where(last, 2.0 * pair, roll_above(edge_t))
     new_p = bp - scale * ((edge_t_above - edge_t) - (emf[2, row + 2] - emf[2, row]))
-    bout[2, row] = new_p[:cols]
+    bout[2, row] = new_p[:cols] - bout[2, row]
     edge_p = emf[1, row] + emf[1, row + 1]
     edge_p_above = jnp.where(last, 2.0 * (emf[0, row] + emf[0, row + 1]), roll_above(edge_p))
     edge_r = emf[2, row] + emf[2, row + 1]
     new_t = ext[6, row] - scale * (
         (roll_right(edge_r) - edge_r) - (edge_p_above - edge_p)
     )
-    bout[1, row] = new_t[:cols]
+    bout[1, row] = new_t[:cols] - bout[1, row]
 
 
 def split(x):
@@ -180,6 +180,8 @@
     both = pl.ds(0, 2)
     modes = pl.ds(0, 2 * KMAX)
     table_loads = [
+        pltpu.make_async_copy(density, dout, load_sem.at[6]),
+        pltpu.make_async_copy(bfield, bout, load_sem.at[7]),
         pltpu.make_async_copy(fwd_hbm.at[both, modes, mine], fwd, load_sem.at[3]),
         pltpu.make_async_copy(back_hbm.at[both, near], back.at[0], load_sem.at[4]),
         pltpu.make_async_copy(back_hbm.at[both, far], back.at[1], load_sem.at[5]),
@@ -546,7 +548,7 @@
     any_space = pl.BlockSpec(memory_space=pl.ANY)
     f32, bf16 = jnp.float32, jnp.bfloat16
     dma = pltpu.SemaphoreType.DMA
-    return pl.pallas_call(
+    density_change, field_change = pl.pallas_call(
         functools.partial(kernel, n, nt, rows, cols),
         out_shape=(
             jax.ShapeDtypeStruct(density.shape, f32),
@@ -572,7 +574,7 @@
             pltpu.VMEM((CHANNELS + 1, rows, radial), f32),
             pltpu.VMEM((CHANNELS, rows, radial), f32),
             pltpu.VMEM((CHANNELS + 1, rows, radial), f32),
-            dma((6,)),
+            dma((8,)),
             dma((HUBS, groups)),
             dma((groups, half_n)),
             dma((groups,)),
@@ -593,6 +595,7 @@
         ),
         name="substep",
     )(density, velocity, bfield, levels, jnp.asarray(forward), jnp.asarray(back))
+    return density + density_change, bfield + field_change
 
 
 def solution(mesh):

time: 51.4 us -> 52.1 us (1.014)
  other arithmetic: 0 us -> 3.4 us
  local copies, waits for them, and re-layouts: 3.18 us -> 0.01 us
    add x0 -> x2, other arithmetic: none -> 3.4 us  [local(): return (density + density_change, bfield + field_change)]
    unnamed x4 -> x6, local copies, waits for them, and re-layouts: 3.18 us -> 0.01 us
where the time goes in v9:
time: 52.1 us; the launch traced here: 51.9 us
  Pallas kernels  47.8 us (92%)
  other arithmetic  3.4 us (7%)
  between operations  0.67 us (1%)
    pallas_call x1, Pallas kernels, local(): pl.pallas_call(functools.partial(kernel, n, nt, rows, cols), out_shape=(j...  47.8 us
    add x2, other arithmetic, local(): return (density + density_change, bfield + field_change)  3.4 us

profile of v9, /device:TPU:0, one launch (start us, length us, event | category | flops | bytes accessed | tf_op | source)
XLA Modules:
  0.0 51.9 jit_solution(18350624148537488592)
XLA Ops:
  0.6 0.0 copy-start.1
  0.6 47.8 %substep.1 = (f32[2,8,96,128]{3,2,1,0:T(8,128)}, f32[3,8,96,128]{3,2,1,0:T(8,128)}) custom-call(f32[2,8,96,128]{3,2,1,0:T(8,128)} %density.1, f32[3,8,96,128]{3,2,1,0:T(8,128)} %velocity.1, f32[3,8,96,128]{3,2,1,0:T(8,128)} %bfield.1, s32[2,4]{1,0:T(2,128)} %levels.1, bf16[2,256,768]{2,1,0:T(8,128)(2,1)} %constant.4.clone.fwd_hbm, ...), custom_call_target="tpu_custom_call" | custom-call | tf_op jit(solution)/shard_map/substep/pallas_call | solution.py:551
  48.5 0.0 copy-done.1
  48.5 0.0 copy-start
  48.5 0.0 copy-start.2
  48.5 2.3 %add.6 = f32[2,8,96,128]{3,2,1,0:T(8,128)} add(f32[2,8,96,128]{3,2,1,0:T(8,128)S(1)} %copy-done.1, f32[2,8,96,128]{3,2,1,0:T(8,128)} %get-tuple-element.4) | non-fusion elementwise | flops 196608 | bytes 2359296 | tf_op jit(solution)/shard_map/add | solution.py:598
  50.8 0.0 copy-done
  50.8 0.0 copy-done.2
  50.8 1.1 %add.7 = f32[3,8,96,128]{3,2,1,0:T(8,128)} add(f32[3,8,96,128]{3,2,1,0:T(8,128)S(1)} %copy-done, f32[3,8,96,128]{3,2,1,0:T(8,128)S(1)} %copy-done.2) | non-fusion elementwise | flops 294912 | bytes 3538944 | tf_op jit(solution)/shard_map/add | solution.py:598
Async XLA Ops:
  0.6 47.8 %copy-start.1 = (f32[2,8,96,128]{3,2,1,0:T(8,128)S(1)}, f32[2,8,96,128]{3,2,1,0:T(8,128)}, u32[]{:S(2)}) copy-start(f32[2,8,96,128]{3,2,1,0:T(8,128)} %density.1) | copy-start | bytes 2359300
  48.5 2.3 %copy-start = (f32[3,8,96,128]{3,2,1,0:T(8,128)S(1)}, f32[3,8,96,128]{3,2,1,0:T(8,128)}, u32[]{:S(2)}) copy-start(f32[3,8,96,128]{3,2,1,0:T(8,128)} %bfield.1) | copy-start | bytes 3538948
  48.5 2.3 %copy-start.2 = (f32[3,8,96,128]{3,2,1,0:T(8,128)S(1)}, f32[3,8,96,128]{3,2,1,0:T(8,128)}, u32[]{:S(2)}) copy-start(f32[3,8,96,128]{3,2,1,0:T(8,128)} %get-tuple-element.5) | copy-start | bytes 3538948
